TPU v7x, 32 devices: a whole 2x2x4 slice. The times are simulated.
32 devices in a mesh: parts: 2 (over y), leaf: 8 (over z, x), sub: 2 (over core).
Axes of the slice: x: 2, y: 2, z: 4, core: 2. Of those that a mesh axis runs over, the one named last changes fastest.
Arguments:
- vectors: float32 [16, 65536], P(None, ('parts', 'leaf', 'sub')), parts along dimension 1, may hold values from -6 to 6
- basis: float32 [1024, 32, 64], P(('parts', 'leaf', 'sub')), parts along dimension 0, may hold values from -0.75 to 0.75
- trans: float32 [32, 31, 2, 32, 32], P(('parts', 'leaf', 'sub')), parts along dimension 0, may hold values from -0.875 to 0.875
- upper_trans: float32 [30, 2, 32, 32], P('parts'), parts along dimension 0, may hold values from -0.875 to 0.875
- upper_coup: float32 [60, 32, 32], P('parts'), parts along dimension 0, may hold values from -1 to 1
- send_node: int32 [32, 16, 4], P(('parts', 'leaf', 'sub')), parts along dimension 0, may hold values from 0 to 62, as said below
- send_count: int32 [32, 16], P(('parts', 'leaf', 'sub')), parts along dimension 0, may hold values from 1 to 4, as said below
- coup_tgt: int32 [32, 16, 4], P(('parts', 'leaf', 'sub')), parts along dimension 0, may hold values from 0 to 62, as said below
- coup_mat: float32 [32, 16, 4, 32, 32], P(('parts', 'leaf', 'sub')), parts along dimension 0, may hold values from -1 to 1
- near_src: int32 [1024, 9], P(('parts', 'leaf', 'sub')), parts along dimension 0, may hold values from 0 to 511, as said below
- near_count: int32 [1024], P(('parts', 'leaf', 'sub')), parts along dimension 0, may hold values from 1 to 9
- near_mat: float32 [1024, 9, 64, 64], P(('parts', 'leaf', 'sub')), parts along dimension 0, may hold values from -0.75 to 0.75
Outputs:
- product: float32 [16, 65536], P(None, ('parts', 'leaf', 'sub')), parts along dimension 1
There are 2 independent parts, one for each index of `parts`. A program takes and returns all parts, laid end to end along the dimension named above; each array names one. Nothing has to cross between parts.
Inputs may be any that keep to these rules, and one draw needn't show every extreme that they name: `send_node`: entry [s, t, j] is a node number of branch s, on the same tree level as node coup_tgt[t, s, j] of branch t. `send_count`: in every draw some branch receives 4 live slots from every branch. `coup_tgt`: A node number of branch t. near_src[l, i] differs from l by at most 16.
All inputs are finite; a program needn't handle non-finite values.
Results may differ from a plain program's by a relative error of at most 0.0003.
Values sent between devices are 32-bit elements; how exact they have to be, the bound alone decides.
No kernel may reach another device: no remote copies, remote signals or barrier semaphores. Data moves between devices by JAX's collectives and lax.ppermute only.
A program may use at most 128 MiB of HBM per device.

v0:
```python
import jax
import jax.numpy as jnp
from jax import lax
from jax.sharding import PartitionSpec as P


def from_partner(value, axis, apart):
    mask = 2**apart
    pairs = [(source, source ^ mask) for source in range(lax.axis_size(axis))]
    return lax.ppermute(value, axis, pairs)


def with_halo(block, sides, width):
    for axis, dim in sides:
        count = lax.axis_size(axis)
        forward = [(i, i + 1) for i in range(count - 1)]
        backward = [(target, source) for source, target in forward]
        low = lax.ppermute(
            lax.slice_in_dim(block, block.shape[dim] - width, None, axis=dim), axis, forward
        )
        high = lax.ppermute(lax.slice_in_dim(block, 0, width, axis=dim), axis, backward)
        block = jnp.concatenate([low, block, high], axis=dim)
    return block


def contract(formula, first, second):
    return jnp.einsum(formula, first, second, precision=lax.Precision.HIGHEST)


def pairwise_upper(top, upper_trans, upper_coup, members, position):
    height = members.bit_length() - 1
    current = top
    couplings = []
    for j in range(height):
        partner = from_partner(current, ("leaf", "sub"), j)
        branch_node = position >> j
        coupler = lax.dynamic_index_in_dim(
            upper_coup, 2 * members - 2 * (members >> j) + branch_node, 0, keepdims=False
        )
        couplings.append(contract("ab,bv->av", coupler, partner))
        if j + 1 < height:
            is_first = branch_node % 2 == 0
            first_child = jnp.where(is_first, current, partner)
            second_child = jnp.where(is_first, partner, current)
            mixer = lax.dynamic_index_in_dim(
                upper_trans, members - (members >> j) + (position >> j + 1), 0, keepdims=False
            )
            current = contract("ab,bv->av", mixer[0], first_child) + contract(
                "ab,bv->av", mixer[1], second_child
            )
    result = couplings[height - 1]
    for j in range(height - 1, 0, -1):
        mixer = lax.dynamic_index_in_dim(
            upper_trans, members - (members >> j - 1) + (position >> j), 0, keepdims=False
        )
        chosen = lax.dynamic_index_in_dim(mixer, (position >> j - 1) % 2, 0, keepdims=False)
        result = couplings[j - 1] + contract("ab,av->bv", chosen, result)
    return result


def local_up(leaf_coef, trans):
    layers = [leaf_coef]
    offset = 0
    number = leaf_coef.shape[-3] // 2
    while number >= 1:
        last = layers[-1]
        children = last.reshape(last.shape[:-3] + (number, 2) + last.shape[-2:])
        layers.append(
            contract(
                "...ncab,...ncbv->...nav", trans[..., offset : offset + number, :, :, :], children
            )
        )
        offset = offset + number
        number = number // 2
    return jnp.concatenate(layers, axis=-3)


def local_down(node_terms, trans):
    nodes = node_terms.shape[-3]
    leaves = (nodes + 1) // 2
    number = 1
    result = node_terms[..., nodes - 1 : nodes, :, :]
    while number < leaves:
        toffset = leaves - 2 * number
        spread = contract(
            "...ncab,...nav->...ncbv", trans[..., toffset : toffset + number, :, :, :], result
        )
        doubled = 2 * number
        noffset = 2 * leaves - 2 * doubled
        result = node_terms[..., noffset : noffset + doubled, :, :] + spread.reshape(
            spread.shape[:-4] + (doubled,) + spread.shape[-2:]
        )
        number = doubled
    return result


def body(
    vectors,
    basis,
    trans,
    upper_trans,
    upper_coup,
    send_node,
    send_count,
    coup_tgt,
    coup_mat,
    near_src,
    near_count,
    near_mat,
):
    vec_size = vectors.shape[0]
    leaf_dev, rank_size, leaf_size = basis.shape
    members = lax.axis_size(("leaf", "sub"))
    position = lax.axis_index(("leaf", "sub"))
    nodes_dev = 2 * leaf_dev - 1
    slots_cap = send_node.shape[2]
    near_slots = near_src.shape[1]
    leaf_values = vectors.reshape(vec_size, leaf_dev, leaf_size)
    halo_width = leaf_dev // 2
    padded = with_halo(leaf_values, ((("leaf", "sub"), 1),), halo_width)
    leaf_coef = contract("lrp,vlp->lrv", basis, leaf_values)
    nodes_all = local_up(leaf_coef, trans[0])
    picked = nodes_all[send_node[0]]
    live = (jnp.arange(slots_cap, dtype=jnp.int32)[None, :] < send_count[0][:, None]).astype(
        jnp.float32
    )
    outgoing = (picked * live[:, :, None, None]).reshape(members, slots_cap, rank_size * vec_size)
    incoming = lax.all_to_all(outgoing, ("leaf", "sub"), split_axis=0, concat_axis=0, tiled=True)
    incoming = incoming.reshape(members, slots_cap, rank_size, vec_size)
    top = nodes_all[nodes_dev - 1]
    top_term = pairwise_upper(top, upper_trans, upper_coup, members, position)
    pieces = contract("scab,scbv->scav", coup_mat[0], incoming)
    selector = (
        coup_tgt[0].reshape(-1)[:, None] == jnp.arange(nodes_dev, dtype=jnp.int32)[None, :]
    ).astype(jnp.float32)
    far_terms = contract(
        "mn,mk->nk", selector, pieces.reshape(members * slots_cap, rank_size * vec_size)
    )
    far_terms = far_terms.reshape(nodes_dev, rank_size, vec_size)
    far_terms = far_terms.at[nodes_dev - 1].add(top_term)
    leaf_terms = local_down(far_terms, trans[0])
    far_part = contract("lrp,lrv->vlp", basis, leaf_terms)
    local_index = near_src - position * leaf_dev + halo_width
    live_near = (jnp.arange(near_slots, dtype=jnp.int32)[None, :] < near_count[:, None]).astype(
        jnp.float32
    )
    neighbours = jnp.take(padded, local_index, axis=1) * live_near[None, :, :, None]
    near_part = contract("lnpq,vlnq->vlp", near_mat, neighbours)
    return (far_part + near_part).reshape(vec_size, leaf_dev * leaf_size)


def solution(mesh):
    return jax.shard_map(
        body,
        mesh=mesh,
        in_specs=(
            P(None, ("parts", "leaf", "sub")),
            P(("parts", "leaf", "sub"), None, None),
            P(("parts", "leaf", "sub"), None, None, None, None),
            P("parts", None, None, None),
            P("parts", None, None),
            P(("parts", "leaf", "sub"), None, None),
            P(("parts", "leaf", "sub"), None),
            P(("parts", "leaf", "sub"), None, None),
            P(("parts", "leaf", "sub"), None, None, None, None),
            P(("parts", "leaf", "sub"), None),
            P(("parts", "leaf", "sub")),
            P(("parts", "leaf", "sub"), None, None, None),
        ),
        out_specs=P(None, ("parts", "leaf", "sub")),
        check_vma=False,
    )
```

profile of v0, /device:TPU:0, one launch (start us, length us, event | category | flops | bytes accessed | tf_op | source)
XLA Modules:
  0.0 77.6 jit_solution(12730935034397846312)
XLA Ops:
  0.0 1.1 %reshape.193 = f32[16,32,64]{2,1,0:T(8,128)S(1)} reshape(f32[16,2048]{1,0:T(8,128)} %param.14) | data formatting | bytes 262144 | tf_op jit(solution)/shard_map/reshape | solution.py:118
  1.1 2.1 %constant_dynamic-update-slice_fusion.2 = (f32[63,32,16]{1,2,0:T(8,128)S(1)}, f32[32,32,16]{1,2,0:T(8,128)S(1)}) fusion(f32[32,32,64]{2,1,0:T(8,128)} %param.15, f32[16,32,64]{2,1,0:T(8,128)S(1)} %reshape.193), kind=kOutput, calls=%fused_computation.104 | convolution fusion | flops 12582911 | bytes 917504 | tf_op jit(solution)/shard_map/lrp,vlp->lrv/dot_general | solution.py:27
  3.2 1.6 %bitcast_dynamic-update-slice_fusion = (f32[63,32,16]{1,2,0:T(8,128)S(1)}, f32[16,16,32,1]{2,1,3,0:T(8,128)S(1)}) fusion(f32[63,32,16]{1,2,0:T(8,128)S(1)} %get-tuple-element.21, f32[16,2,32,16]{2,3,1,0:T(8,128)S(1)} %bitcast.203, f32[1,31,2,32,32]{4,3,2,1,0:T(8,128)} %param.16), kind=kOutput, calls=%fused_computation.48 | convolution fusion | flops 6291456 | bytes 1048576 | tf_op jit(solution)/shard_map/...ncab,...ncbv->...nav/dot_general | solution.py:27
  4.8 1.3 %bitcast_dynamic-update-slice_fusion.1 = (f32[63,32,16]{1,2,0:T(8,128)S(1)}, f32[8,16,32,1]{2,1,3,0:T(8,128)S(1)}) fusion(f32[63,32,16]{1,2,0:T(8,128)S(1)} %get-tuple-element.23, f32[8,2,32,16]{2,3,1,0:T(8,128)S(1)} %bitcast.205, f32[1,31,2,32,32]{4,3,2,1,0:T(8,128)} %param.16), kind=kOutput, calls=%fused_computation.56 | convolution fusion | flops 3145728 | bytes 524288 | tf_op jit(solution)/shard_map/...ncab,...ncbv->...nav/dot_general | solution.py:27
  6.1 1.1 %bitcast_dynamic-update-slice_fusion.2 = (f32[63,32,16]{1,2,0:T(8,128)S(1)}, f32[4,16,32,1]{2,1,3,0:T(8,128)S(1)}) fusion(f32[63,32,16]{1,2,0:T(8,128)S(1)} %get-tuple-element.25, f32[4,2,32,16]{2,3,1,0:T(8,128)S(1)} %bitcast.206, f32[1,31,2,32,32]{4,3,2,1,0:T(8,128)} %param.16), kind=kOutput, calls=%fused_computation.66 | convolution fusion | flops 1572864 | bytes 262144 | tf_op jit(solution)/shard_map/...ncab,...ncbv->...nav/dot_general | solution.py:27
  7.3 1.0 %constant_dynamic-update-slice_fusion.1 = (f32[63,32,16]{1,2,0:T(8,128)S(1)}, f32[2,32,16]{1,2,0:T(8,128)S(1)}) fusion(f32[63,32,16]{1,2,0:T(8,128)S(1)} %get-tuple-element.27, f32[2,2,32,16]{2,3,1,0:T(8,128)S(1)} %bitcast.207, f32[1,31,2,32,32]{4,3,2,1,0:T(8,128)} %param.16), kind=kOutput, calls=%fused_computation.103 | convolution fusion | flops 786432 | bytes 131072 | tf_op jit(solution)/shard_map/...ncab,...ncbv->...nav/dot_general | solution.py:27
  8.3 0.9 %constant_dynamic-update-slice_fusion = (f32[63,32,16]{1,2,0:T(8,128)S(1)}, f32[16,32,1]{1,0,2:T(8,128)S(1)}) fusion(f32[63,32,16]{1,2,0:T(8,128)S(1)} %get-tuple-element.29, f32[2,32,16]{1,2,0:T(8,128)S(1)} %get-tuple-element.30, f32[1,31,2,32,32]{4,3,2,1,0:T(8,128)} %param.16), kind=kOutput, calls=%fused_computation.102 | convolution fusion | flops 393216 | bytes 65536 | tf_op jit(solution)/shard_map/...ncab,...ncbv->...nav/dot_general | solution.py:27
  9.2 0.5 collective-permute-start
  9.9 0.6 gather_fusion
  10.6 0.4 copy.77
  10.9 0.6 gather.10
  11.6 0.7 broadcast_multiply_fusion
  12.3 7.0 %all-to-all-start = ((f32[16,4,512]{2,1,0:T(4,128)}), f32[16,4,512]{2,1,0:T(4,128)S(1)}, u32[]{:S(2)}, u32[]{:S(2)}) async-start(f32[16,4,512]{2,1,0:T(4,128)} %broadcast_multiply_fusion), calls=%async_computation | async-start | bytes 262144 | tf_op jit(solution)/shard_map/all_to_all | solution.py:128
  19.3 0.2 copy.75
  19.5 2.3 %collective-permute-start.4 = (f32[16,16,64]{2,0,1:T(8,128)S(1)}, f32[16,16,64]{2,0,1:T(8,128)S(1)}, u32[]{:S(2)}, u32[]{:S(2)}) collective-permute-start(f32[16,16,64]{2,0,1:T(8,128)S(1)} %get-tuple-element.19), channel_id=1, source_target_pairs={{0,1},{1,2},{2,3},{3,4},{4,5},{5,6},{6,7},{7,8},{8,9},{9,10},{10,1... | collective-permute-start | bytes 196616 | tf_op jit(solution)/shard_map/ppermute | solution.py:18
  21.9 1.5 %collective-permute-start.5 = (f32[16,16,64]{2,0,1:T(8,128)S(1)}, f32[16,16,64]{2,0,1:T(8,128)S(1)}, u32[]{:S(2)}, u32[]{:S(2)}) collective-permute-start(f32[16,16,64]{2,0,1:T(8,128)S(1)} %get-tuple-element.20), channel_id=1, source_target_pairs={{1,0},{2,1},{3,2},{4,3},{5,4},{6,5},{7,6},{8,7},{9,8},{10,9},{11,1... | collective-permute-start | bytes 196616 | tf_op jit(solution)/shard_map/ppermute | solution.py:21
  23.4 0.9 %fusion.53 = f32[32,16]{0,1:T(8,128)S(1)} fusion(f32[15,2,32,32]{3,2,1,0:T(8,128)} %param.17, s32[]{:T(128)S(6)} %select_n.122, s32[]{:T(128)S(6)} %add.198, f32[32,16]{0,1:T(8,128)S(1)} %collective-permute-done, pred[]{:T(512)S(6)} %eq.35, f32[16,32,1]{1,0,2:T(8,128)S(1)} %get-tuple-element.32), kind=kOutput, calls=%fused_computation.79 | convolution fusion | flops 197120 | bytes 22537 | tf_op jit(solution)/shard_map/ab,bv->av/dot_general | solution.py:27
  24.2 0.9 %convolution_add_fusion.5 = f32[32,16]{0,1:T(8,128)S(1)} fusion(f32[32,16]{0,1:T(8,128)S(1)} %fusion.53, f32[15,2,32,32]{3,2,1,0:T(8,128)} %param.17, s32[]{:T(128)S(6)} %select_n.122, f32[32,16]{0,1:T(8,128)S(1)} %collective-permute-done, pred[]{:T(512)S(6)} %eq.35, f32[16,32,1]{1,0,2:T(8,128)S(1)} %get-tuple-element.32), kind=kOutput, calls=%fused_computation.18 | convolution fusion | flops 197632 | bytes 24581 | tf_op jit(solution)/shard_map/ab,bv->av/dot_general | solution.py:27
  25.1 3.9 %collective-permute-start.1 = (f32[32,16]{0,1:T(8,128)S(1)}, f32[32,16]{0,1:T(8,128)S(1)}, u32[]{:S(2)}, u32[]{:S(2)}) collective-permute-start(f32[32,16]{0,1:T(8,128)S(1)} %convolution_add_fusion.5), channel_id=1, source_target_pairs={{0,2},{1,3},{2,0},{3,1},{4,6},{5,7},{6,4},{7,5},{8,10},{9,11},{10,... | collective-permute-start | bytes 6152 | tf_op jit(solution)/shard_map/ppermute | solution.py:10
  29.2 0.1 reshape.218
  29.3 1.4 %collective-permute-done.1 = f32[32,16]{0,1:T(8,128)S(1)} collective-permute-done((f32[32,16]{0,1:T(8,128)S(1)}, f32[32,16]{0,1:T(8,128)S(1)}, u32[]{:S(2)}, u32[]{:S(2)}) %collective-permute-start.1) | collective-permute-done | bytes 2080 | tf_op jit(solution)/shard_map/ppermute | solution.py:10
  30.6 0.8 %fusion.52 = f32[32,16]{0,1:T(8,128)S(1)} fusion(f32[15,2,32,32]{3,2,1,0:T(8,128)} %param.17, s32[]{:T(128)S(6)} %select_n.131, s32[]{:T(128)S(6)} %add.198, f32[32,16]{0,1:T(8,128)S(1)} %collective-permute-done.1, f32[32,16]{0,1:T(8,128)S(1)} %convolution_add_fusion.5, pred[]{:T(512)S(6)} %eq.36), kind=kOutput, calls=%fused_computation.76 | convolution fusion | flops 197120 | bytes 22537 | tf_op jit(solution)/shard_map/ab,bv->av/dot_general | solution.py:27
  31.5 0.9 %convolution_add_fusion.3 = f32[32,16]{0,1:T(8,128)S(1)} fusion(f32[32,16]{0,1:T(8,128)S(1)} %fusion.52, f32[15,2,32,32]{3,2,1,0:T(8,128)} %param.17, s32[]{:T(128)S(6)} %select_n.131, f32[32,16]{0,1:T(8,128)S(1)} %convolution_add_fusion.5, f32[32,16]{0,1:T(8,128)S(1)} %collective-permute-done.1, pred[]{:T(512)S(6)} %eq.36), kind=kOutput, calls=%fused_computation.16 | convolution fusion | flops 197632 | bytes 24581 | tf_op jit(solution)/shard_map/ab,bv->av/dot_general | solution.py:27
  32.4 2.9 %collective-permute-start.2 = (f32[32,16]{0,1:T(8,128)S(1)}, f32[32,16]{0,1:T(8,128)S(1)}, u32[]{:S(2)}, u32[]{:S(2)}) collective-permute-start(f32[32,16]{0,1:T(8,128)S(1)} %convolution_add_fusion.3), channel_id=1, source_target_pairs={{0,4},{1,5},{2,6},{3,7},{4,0},{5,1},{6,2},{7,3},{8,12},{9,13},{10,... | collective-permute-start | bytes 6152 | tf_op jit(solution)/shard_map/ppermute | solution.py:10
  35.3 1.6 %collective-permute-done.2 = f32[32,16]{0,1:T(8,128)S(1)} collective-permute-done((f32[32,16]{0,1:T(8,128)S(1)}, f32[32,16]{0,1:T(8,128)S(1)}, u32[]{:S(2)}, u32[]{:S(2)}) %collective-permute-start.2) | collective-permute-done | bytes 2080 | tf_op jit(solution)/shard_map/ppermute | solution.py:10
  36.9 0.8 %fusion.51 = f32[32,16]{0,1:T(8,128)S(1)} fusion(f32[15,2,32,32]{3,2,1,0:T(8,128)} %param.17, s32[]{:T(128)S(6)} %select_n.140, s32[]{:T(128)S(6)} %add.198, f32[32,16]{0,1:T(8,128)S(1)} %collective-permute-done.2, f32[32,16]{0,1:T(8,128)S(1)} %convolution_add_fusion.3, pred[]{:T(512)S(6)} %eq.37), kind=kOutput, calls=%fused_computation.73 | convolution fusion | flops 197120 | bytes 22537 | tf_op jit(solution)/shard_map/ab,bv->av/dot_general | solution.py:27
  37.8 0.9 %convolution_add_fusion.1 = f32[32,16]{0,1:T(8,128)S(1)} fusion(f32[32,16]{0,1:T(8,128)S(1)} %fusion.51, f32[15,2,32,32]{3,2,1,0:T(8,128)} %param.17, s32[]{:T(128)S(6)} %select_n.140, f32[32,16]{0,1:T(8,128)S(1)} %convolution_add_fusion.3, f32[32,16]{0,1:T(8,128)S(1)} %collective-permute-done.2, pred[]{:T(512)S(6)} %eq.37), kind=kOutput, calls=%fused_computation.14 | convolution fusion | flops 197632 | bytes 24581 | tf_op jit(solution)/shard_map/ab,bv->av/dot_general | solution.py:27
  38.7 2.9 %collective-permute-start.3 = (f32[32,16]{0,1:T(8,128)S(1)}, f32[32,16]{0,1:T(8,128)S(1)}, u32[]{:S(2)}, u32[]{:S(2)}) collective-permute-start(f32[32,16]{0,1:T(8,128)S(1)} %convolution_add_fusion.1), channel_id=1, source_target_pairs={{0,8},{1,9},{2,10},{3,11},{4,12},{5,13},{6,14},{7,15},{8,0},{9,1},... | collective-permute-start | bytes 6152 | tf_op jit(solution)/shard_map/ppermute | solution.py:10
  41.9 1.4 %collective-permute-done.3 = f32[32,16]{0,1:T(8,128)S(1)} collective-permute-done((f32[32,16]{0,1:T(8,128)S(1)}, f32[32,16]{0,1:T(8,128)S(1)}, u32[]{:S(2)}, u32[]{:S(2)}) %collective-permute-start.3) | collective-permute-done | bytes 2080 | tf_op jit(solution)/shard_map/ppermute | solution.py:10
  43.2 0.8 %fusion.54 = f32[32,16]{0,1:T(8,128)S(1)} fusion(f32[32,16]{0,1:T(8,128)S(1)} %collective-permute-done.3, f32[30,32,32]{2,1,0:T(8,128)} %param.18, s32[]{:T(128)S(6)} %select_n.145), kind=kOutput, calls=%fused_computation.81 | convolution fusion | flops 196608 | bytes 20484 | tf_op jit(solution)/shard_map/ab,bv->av/dot_general | solution.py:27
  44.1 0.9 %fusion.56 = f32[32,16]{0,1:T(8,128)S(1)} fusion(f32[32,16]{0,1:T(8,128)S(1)} %fusion.54, f32[15,2,32,32]{3,2,1,0:T(8,128)} %param.17, s32[]{:T(128)S(6)} %select_n.141, s32[]{:T(128)S(6)} %select_n.144), kind=kOutput, calls=%fused_computation.83 | convolution fusion | flops 196608 | bytes 20488 | tf_op jit(solution)/shard_map/ab,av->bv/dot_general | solution.py:27
  45.0 0.9 %convolution_add_fusion.2 = f32[32,16]{0,1:T(8,128)S(1)} fusion(f32[32,16]{0,1:T(8,128)S(1)} %fusion.56, f32[32,16]{0,1:T(8,128)S(1)} %collective-permute-done.2, f32[30,32,32]{2,1,0:T(8,128)} %param.18, s32[]{:T(128)S(6)} %select_n.136), kind=kOutput, calls=%fused_computation.15 | convolution fusion | flops 197120 | bytes 22532 | tf_op jit(solution)/shard_map/ab,bv->av/dot_general | solution.py:27
  45.8 0.9 %fusion.59 = f32[32,16]{0,1:T(8,128)S(1)} fusion(f32[32,16]{0,1:T(8,128)S(1)} %convolution_add_fusion.2, f32[15,2,32,32]{3,2,1,0:T(8,128)} %param.17, s32[]{:T(128)S(6)} %select_n.132, s32[]{:T(128)S(6)} %select_n.135), kind=kOutput, calls=%fused_computation.86 | convolution fusion | flops 196608 | bytes 20488 | tf_op jit(solution)/shard_map/ab,av->bv/dot_general | solution.py:27
  46.7 0.9 %convolution_add_fusion.4 = f32[32,16]{0,1:T(8,128)S(1)} fusion(f32[32,16]{0,1:T(8,128)S(1)} %fusion.59, f32[32,16]{0,1:T(8,128)S(1)} %collective-permute-done.1, f32[30,32,32]{2,1,0:T(8,128)} %param.18, s32[]{:T(128)S(6)} %select_n.127), kind=kOutput, calls=%fused_computation.17 | convolution fusion | flops 197120 | bytes 22532 | tf_op jit(solution)/shard_map/ab,bv->av/dot_general | solution.py:27
  47.5 0.9 %fusion.62 = f32[32,16]{0,1:T(8,128)S(1)} fusion(f32[32,16]{0,1:T(8,128)S(1)} %convolution_add_fusion.4, f32[15,2,32,32]{3,2,1,0:T(8,128)} %param.17, s32[]{:T(128)S(6)} %select_n.123, s32[]{:T(128)S(6)} %select_n.126), kind=kOutput, calls=%fused_computation.89 | convolution fusion | flops 196608 | bytes 20488 | tf_op jit(solution)/shard_map/ab,av->bv/dot_general | solution.py:27
  48.4 0.9 %fusion.11 = f32[1,32,16]{1,2,0:T(8,128)S(1)} fusion(f32[32,16]{0,1:T(8,128)S(1)} %fusion.62, f32[32,16]{0,1:T(8,128)S(1)} %collective-permute-done, f32[30,32,32]{2,1,0:T(8,128)} %param.18, s32[]{:T(128)S(6)} %select_n.121), kind=kOutput, calls=%fused_computation.20 | convolution fusion | flops 197120 | bytes 22532 | tf_op jit(solution)/shard_map/ab,bv->av/dot_general | solution.py:27
  49.3 0.9 %copy.86 = f32[1,32,16]{0,1,2:T(8,128)} copy(f32[1,32,16]{1,2,0:T(8,128)S(1)} %fusion.11) | data formatting | bytes 4096 | tf_op jit(solution)/shard_map/reshape.39
  50.2 2.6 %gather_fusion.1 = f32[288,16,64]{2,1,0:T(8,128)} fusion(f32[16,64,64]{2,0,1:T(8,128)S(1)} %pad_maximum_fusion, s32[1024]{0:T(1024)S(1)} %pad_clamp_fusion), kind=kCustom, calls=%fused_computation.1 | custom fusion | bytes 2360448 | tf_op jit(solution)/shard_map/jit(_take)/gather | solution.py:147
  52.8 11.5 %fusion.8 = f32[32,16,64]{2,1,0:T(8,128)S(1)} fusion(f32[32,9,64,64]{3,2,1,0:T(8,128)} %param.25, f32[32,9,16,64]{3,2,1,0:T(8,128)} %bitcast.200, f32[32,9]{1,0:T(8,128)S(1)} %fusion.73, pred[32,9]{1,0:T(8,128)(4,1)S(1)} %copy.91), kind=kOutput, calls=%fused_computation.12 | convolution fusion | flops 227082240 | bytes 6030752 | tf_op jit(solution)/shard_map/lnpq,vlnq->vlp/dot_general | solution.py:27
  64.3 0.4 reshape.240
  64.7 1.8 %convolution_bitcast_fusion = f32[16,4,32,16]{2,3,1,0:T(8,128)S(1)} fusion(f32[16,4,32,16]{3,2,1,0:T(8,128)S(1)} %reshape.240, f32[1,16,4,32,32]{4,3,2,1,0:T(8,128)S(1)} %copy-done), kind=kOutput, calls=%fused_computation.6 | convolution fusion | flops 12582912 | bytes 524288 | tf_op jit(solution)/shard_map/scab,scbv->scav/dot_general | solution.py:27
  66.5 0.4 copy.80
  66.9 0.6 reshape.200
  67.5 0.1 copy.81
  67.6 0.3 fusion.25
  68.0 0.8 %slice.131 = f32[4,32,16]{0,1,2:T(8,128)} slice(f32[63,32,16]{0,1,2:T(8,128)S(1)} %fusion.25), slice={[56:60], [0:32], [0:16]} | slice | bytes 16384 | tf_op jit(solution)/shard_map/slice | solution.py:90
  68.8 0.1 slice.130
  68.9 0.8 %slice.129 = f32[16,32,16]{0,1,2:T(8,128)} slice(f32[63,32,16]{0,1,2:T(8,128)S(1)} %fusion.25), slice={[32:48], [0:32], [0:16]} | slice | bytes 65536 | tf_op jit(solution)/shard_map/slice | solution.py:90
  69.8 0.3 fusion.19
  70.0 0.1 fusion.43
  70.2 0.2 copy.87
  70.4 0.1 fusion.20
  70.5 0.2 copy.102
  70.7 0.2 fusion.37
  70.8 1.1 %copy.113 = f32[4,32,16]{1,2,0:T(8,128)S(1)} copy(f32[4,32,16]{0,1,2:T(8,128)} %slice.131) | data formatting | bytes 16384
  72.0 0.2 fusion.30
  72.2 0.1 copy.112
  72.3 0.3 fusion.21
  72.6 1.1 %copy.111 = f32[16,32,16]{1,2,0:T(8,128)S(1)} copy(f32[16,32,16]{0,1,2:T(8,128)} %slice.129) | data formatting | bytes 65536
  73.7 1.1 %fusion.13 = f32[16,16,2,32]{3,1,2,0:T(8,128)} fusion(f32[1,31,2,32,32]{4,3,2,1,0:T(8,128)S(1)} %copy-done.1, f32[16,32,16]{1,2,0:T(8,128)S(1)} %bitcast_add_fusion), kind=kOutput, calls=%fused_computation.23 | convolution fusion | flops 6291456 | bytes 720896 | tf_op jit(solution)/shard_map/...ncab,...nav->...ncbv/dot_general | solution.py:27
  74.8 1.1 %copy.89 = f32[32,32,16]{0,1,2:T(8,128)S(1)} copy(f32[32,32,16]{1,2,0:T(8,128)} %bitcast.202) | data formatting | bytes 131072 | tf_op jit(solution)/shard_map/reshape | solution.py:90
  76.0 0.2 copy.90
  76.2 0.6 fusion.7
  76.8 0.8 reshape.207
  (41 shorter events, 1.0 us)
Async XLA Ops:
  0.0 64.7 %copy-start = (f32[1,16,4,32,32]{4,3,2,1,0:T(8,128)S(1)}, f32[1,16,4,32,32]{4,3,2,1,0:T(8,128)}, u32[]{:S(2)}) copy-start(f32[1,16,4,32,32]{4,3,2,1,0:T(8,128)} %param.22) | copy-start | bytes 786436
  0.0 9.7 %copy-start.6 = (s32[1,16,4]{1,2,0:T(4,128)S(1)}, s32[1,16,4]{1,2,0:T(4,128)}, u32[]{:S(2)}) copy-start(s32[1,16,4]{1,2,0:T(4,128)} %param.19) | copy-start | bytes 772
  9.2 14.2 %collective-permute-start = (f32[32,16]{0,1:T(8,128)S(1)}, f32[32,16]{0,1:T(8,128)S(1)}, u32[]{:S(2)}, u32[]{:S(2)}) collective-permute-start(f32[32,16]{0,1:T(8,128)S(1)} %bitcast.208), channel_id=1, source_target_pairs={{0,1},{1,0},{2,3},{3,2},{4,5},{5,4},{6,7},{7,6},{8,9},{9,8},{10,11... | collective-permute-start | bytes 6152 | tf_op jit(solution)/shard_map/ppermute | solution.py:10
  9.9 1.6 %copy-start.7 = (s32[1,16]{1,0:T(1,128)S(1)}, s32[1,16]{1,0:T(1,128)}, u32[]{:S(2)}) copy-start(s32[1,16]{1,0:T(1,128)} %param.20) | copy-start | bytes 196
  10.5 12.8 %copy-start.4 = (s32[32,9]{0,1:T(8,128)S(1)}, s32[32,9]{0,1:T(8,128)}, u32[]{:S(2)}) copy-start(s32[32,9]{0,1:T(8,128)} %param.23) | copy-start | bytes 3460
  10.5 18.5 %copy-start.8 = (s32[32]{0:T(128)S(1)}, s32[32]{0:T(128)}, u32[]{:S(2)}) copy-start(s32[32]{0:T(128)} %param.24) | copy-start | bytes 388
  10.6 31.1 %copy-start.5 = (s32[1,16,4]{1,2,0:T(4,128)S(1)}, s32[1,16,4]{1,2,0:T(4,128)}, u32[]{:S(2)}) copy-start(s32[1,16,4]{1,2,0:T(4,128)} %param.21) | copy-start | bytes 772
  12.3 52.0 %all-to-all-start = ((f32[16,4,512]{2,1,0:T(4,128)}), f32[16,4,512]{2,1,0:T(4,128)S(1)}, u32[]{:S(2)}, u32[]{:S(2)}) async-start(f32[16,4,512]{2,1,0:T(4,128)} %broadcast_multiply_fusion), calls=%async_computation | async-start | bytes 262144 | tf_op jit(solution)/shard_map/all_to_all | solution.py:128
  19.5 30.6 %collective-permute-start.4 = (f32[16,16,64]{2,0,1:T(8,128)S(1)}, f32[16,16,64]{2,0,1:T(8,128)S(1)}, u32[]{:S(2)}, u32[]{:S(2)}) collective-permute-start(f32[16,16,64]{2,0,1:T(8,128)S(1)} %get-tuple-element.19), channel_id=1, source_target_pairs={{0,1},{1,2},{2,3},{3,4},{4,5},{5,6},{6,7},{7,8},{8,9},{9,10},{10,1... | collective-permute-start | bytes 196616 | tf_op jit(solution)/shard_map/ppermute | solution.py:18
  21.9 28.3 %collective-permute-start.5 = (f32[16,16,64]{2,0,1:T(8,128)S(1)}, f32[16,16,64]{2,0,1:T(8,128)S(1)}, u32[]{:S(2)}, u32[]{:S(2)}) collective-permute-start(f32[16,16,64]{2,0,1:T(8,128)S(1)} %get-tuple-element.20), channel_id=1, source_target_pairs={{1,0},{2,1},{3,2},{4,3},{5,4},{6,5},{7,6},{8,7},{9,8},{10,9},{11,1... | collective-permute-start | bytes 196616 | tf_op jit(solution)/shard_map/ppermute | solution.py:21
  25.1 5.5 %collective-permute-start.1 = (f32[32,16]{0,1:T(8,128)S(1)}, f32[32,16]{0,1:T(8,128)S(1)}, u32[]{:S(2)}, u32[]{:S(2)}) collective-permute-start(f32[32,16]{0,1:T(8,128)S(1)} %convolution_add_fusion.5), channel_id=1, source_target_pairs={{0,2},{1,3},{2,0},{3,1},{4,6},{5,7},{6,4},{7,5},{8,10},{9,11},{10,... | collective-permute-start | bytes 6152 | tf_op jit(solution)/shard_map/ppermute | solution.py:10
  32.4 4.6 %collective-permute-start.2 = (f32[32,16]{0,1:T(8,128)S(1)}, f32[32,16]{0,1:T(8,128)S(1)}, u32[]{:S(2)}, u32[]{:S(2)}) collective-permute-start(f32[32,16]{0,1:T(8,128)S(1)} %convolution_add_fusion.3), channel_id=1, source_target_pairs={{0,4},{1,5},{2,6},{3,7},{4,0},{5,1},{6,2},{7,3},{8,12},{9,13},{10,... | collective-permute-start | bytes 6152 | tf_op jit(solution)/shard_map/ppermute | solution.py:10
  38.7 4.6 %collective-permute-start.3 = (f32[32,16]{0,1:T(8,128)S(1)}, f32[32,16]{0,1:T(8,128)S(1)}, u32[]{:S(2)}, u32[]{:S(2)}) collective-permute-start(f32[32,16]{0,1:T(8,128)S(1)} %convolution_add_fusion.1), channel_id=1, source_target_pairs={{0,8},{1,9},{2,10},{3,11},{4,12},{5,13},{6,14},{7,15},{8,0},{9,1},... | collective-permute-start | bytes 6152 | tf_op jit(solution)/shard_map/ppermute | solution.py:10
  66.8 3.2 %copy-start.1 = (f32[1,31,2,32,32]{4,3,2,1,0:T(8,128)S(1)}, f32[1,31,2,32,32]{4,3,2,1,0:T(8,128)}, u32[]{:S(2)}) copy-start(f32[1,31,2,32,32]{4,3,2,1,0:T(8,128)} %param.16) | copy-start | bytes 761860
  67.5 2.3 %copy-start.3 = (f32[1,32,16]{0,1,2:T(8,128)S(1)}, f32[1,32,16]{0,1,2:T(8,128)}, u32[]{:S(2)}) copy-start(f32[1,32,16]{0,1,2:T(8,128)} %copy.86) | copy-start | bytes 6148
  72.0 4.2 %copy-start.2 = (f32[32,32,64]{2,1,0:T(8,128)S(1)}, f32[32,32,64]{2,1,0:T(8,128)}, u32[]{:S(2)}) copy-start(f32[32,32,64]{2,1,0:T(8,128)} %param.15) | copy-start | bytes 786436
where the time goes:
time: 79.1 us; the launch traced here: 77.6 us
  matrix products  35.3 us (45%)
  starting transfers between devices  21.1 us (27%)
  local copies, waits for them, and re-layouts  15.1 us (19%)
  waiting for transfers between devices  4.35 us (5%)
  other arithmetic  1.43 us (2%)
    dot_general x28, matrix products, contract(): return jnp.einsum(formula, first, second, precision=lax.Precision.HIGHEST)  35.3 us
    ppermute x4, starting transfers between devices, from_partner(): return lax.ppermute(value, axis, pairs)  10.3 us
    all_to_all x1, starting transfers between devices, body(): lax.all_to_all(outgoing, ('leaf', 'sub'), split_axis=0, concat_axis=0, ti...  7.02 us
    ppermute x4, waiting for transfers between devices, from_partner(): return lax.ppermute(value, axis, pairs)  4.34 us
    gather x1, local copies, waits for them, and re-layouts, body(): jnp.take(padded, local_index, axis=1) * live_near[None, :, :, None]  2.57 us
    unnamed x22, local copies, waits for them, and re-layouts  2.46 us
    ppermute x1, starting transfers between devices, with_halo(): lax.ppermute(lax.slice_in_dim(block, block.shape[dim] - width, None, axis...  2.32 us
    slice x3, local copies, waits for them, and re-layouts, local_down(): node_terms[..., noffset:noffset + doubled, :, :]  1.8 us
  transfers between devices with their start and end apart: 7, of which 3 were waited for; matrix products, arithmetic and copies ran while one was open for 38% of the time, Pallas kernels for 0%

commit v1 on v0

v1 whole, which is shorter than its diff:
```python
import functools

import jax
import jax.numpy as jnp
from jax import lax
from jax.experimental import pallas as pl
from jax.experimental.pallas import tpu as pltpu
from jax.sharding import PartitionSpec as P

BRANCH = ("leaf", "sub")
LANES = 128
F32 = jnp.float32
BF16 = jnp.bfloat16
MIB = 1 << 20


def split(x):
    high = x.astype(BF16)
    low = (x - high.astype(F32)).astype(BF16)
    return high, low


def contract_nt(a, b):
    return lax.dot_general(a, b, (((1,), (1,)), ((), ())), preferred_element_type=F32)


def contract_nn(a, b):
    return lax.dot_general(a, b, (((1,), (0,)), ((), ())), preferred_element_type=F32)


def contract_tn(a, b):
    return lax.dot_general(a, b, (((0,), (0,)), ((), ())), preferred_element_type=F32)


def times(x, high, low, dot):
    rows = x.shape[0]
    x_high, x_low = split(x)
    both = dot(jnp.concatenate([x_high, x_low], axis=0), high)
    return both[:rows] + both[rows:] + dot(x_high, low)


def product(a, b, dot):
    a_high, a_low = split(a)
    b_high, b_low = split(b)
    return dot(a_high, b_high) + (dot(a_high, b_low) + dot(a_low, b_high))


def lane_part(rows, part):
    return lax.broadcasted_iota(jnp.int32, (rows, LANES), 1) // part


def over(count, body, step=16):
    if count <= step:
        for i in range(count):
            body(i)
    else:

        def several(k, carry):
            for u in range(step):
                body(k * step + u)
            return carry

        lax.fori_loop(0, count // step, several, 0)


def fetch(sources, targets, semaphores):
    copies = []
    for i, (source, target) in enumerate(zip(sources, targets)):
        copies.append(pltpu.make_async_copy(source, target, semaphores.at[i]))
        copies[i].start()
    return copies


def up_kernel(
    members,
    slots,
    vec_far,
    basis_far,
    trans_far,
    send_node_far,
    send_count_far,
    outgoing,
    sub_half,
    cross_half,
    weights,
    vec,
    basis,
    trans,
    send_node,
    send_count,
    rolled,
    semaphores,
):
    arriving = fetch(
        (vec_far, basis_far, trans_far, send_node_far, send_count_far),
        (vec, basis, trans, send_node, send_count),
        semaphores,
    )
    basis_high, basis_low, trans_high, trans_low = (weights.at[i] for i in range(4))
    position = lax.axis_index(BRANCH)
    leaf_dev, rank, leaf_size = basis.shape
    vecs = vec.shape[0]
    arriving[0].wait()
    arriving[1].wait()
    half = vec.shape[1] // 2
    even = position % 2 == 0
    low_half = vec[:, :half]
    high_half = vec[:, half:]
    sub_half[...] = jnp.where(even, high_half, low_half)
    cross_half[...] = jnp.where(even, low_half, high_half)

    for leaf in range(leaf_dev):
        group, q = leaf // 4, leaf % 4
        blank = jnp.zeros((rank, LANES - leaf_size), F32)
        pieces = [basis[leaf], blank] if q % 2 == 0 else [blank, basis[leaf]]
        high, low = split(jnp.concatenate(pieces, axis=1))
        rows = slice(q * rank, (q + 1) * rank)
        here = slice(0, LANES) if q < 2 else slice(LANES, 2 * LANES)
        other = slice(LANES, 2 * LANES) if q < 2 else slice(0, LANES)
        basis_high[group, rows, here] = high
        basis_low[group, rows, here] = low
        basis_high[group, rows, other] = jnp.zeros((rank, LANES), BF16)
        basis_low[group, rows, other] = jnp.zeros((rank, LANES), BF16)
    arriving[2].wait()
    for node in range(leaf_dev):
        group, q = node // 4, node % 4
        rows = slice(q * rank, (q + 1) * rank)
        here = slice(0, LANES) if q < 2 else slice(LANES, 2 * LANES)
        other = slice(LANES, 2 * LANES) if q < 2 else slice(0, LANES)
        if node < leaf_dev - 1:
            pair = [trans[2 * node], trans[2 * node + 1]]
            blank = jnp.zeros((rank, LANES - 2 * rank), F32)
            pieces = pair + [blank] if q % 2 == 0 else [blank] + pair
            high, low = split(jnp.concatenate(pieces, axis=1))
        else:
            high = low = jnp.zeros((rank, LANES), BF16)
        trans_high[group, rows, here] = high
        trans_low[group, rows, here] = low
        trans_high[group, rows, other] = jnp.zeros((rank, LANES), BF16)
        trans_low[group, rows, other] = jnp.zeros((rank, LANES), BF16)

    def keep(group, value):
        for k in range(4):
            rolled[4 * group + k] = value if k == 0 else pltpu.roll(value, k * rank, 1)

    level = []
    for g in range(leaf_dev // 4):
        x = vec[:, 2 * LANES * g : 2 * LANES * (g + 1)]
        level.append(times(x, basis_high[g], basis_low[g], contract_nt))
        keep(g, level[g])
    done = leaf_dev // 4
    weight = 0
    while len(level) > 1:
        nodes = []
        for g in range(len(level) // 2):
            children = jnp.concatenate([level[2 * g], level[2 * g + 1]], axis=1)
            nodes.append(times(children, trans_high[weight], trans_low[weight], contract_nt))
            keep(done, nodes[g])
            weight += 1
            done += 1
        level = nodes
    two = times(level[0], trans_high[weight, :, :LANES], trans_low[weight, :, :LANES], contract_nt)
    top = times(two, trans_high[weight, :, LANES:], trans_low[weight, :, LANES:], contract_nt)
    keep(done, two + top)
    blank_index = 4 * (done + 1)
    rolled[blank_index] = jnp.zeros((vecs, LANES), F32)

    arriving[3].wait()
    arriving[4].wait()
    part = lane_part(vecs, rank)
    few = lane_part(vecs // 2, rank)
    first = position & 3
    second = (position + 1) & 3
    top_rows = jnp.where(
        few == first,
        rolled[4 * done + ((first - 2) & 3), : vecs // 2],
        jnp.where(few == second, rolled[4 * done + ((second - 2) & 3), vecs // 2 :], 0.0),
    )

    def pick(target):
        count = send_count[0, target]
        value = None
        for j in range(slots):
            node = send_node[j, target]
            index = (node >> 2) * 4 + ((j - node) & 3)
            piece = rolled[jnp.where(j < count, index, blank_index)]
            value = piece if value is None else jnp.where(part == j, piece, value)
        outgoing[target, :vecs] = value
        outgoing[target, vecs:] = top_rows

    over(members, pick)


def prepare_kernel(
    members,
    slots,
    coup_mat_far,
    upper_trans_far,
    upper_coup_far,
    far_high,
    far_low,
    coup_mat,
    upper_trans,
    upper_coup,
    semaphores,
):
    arriving = fetch(
        (coup_mat_far, upper_trans_far, upper_coup_far), (coup_mat, upper_trans, upper_coup), semaphores
    )
    position = lax.axis_index(BRANCH)
    for copy in arriving:
        copy.wait()
    rank = coup_mat.shape[1]
    height = members.bit_length() - 1

    def one(source):
        for j in range(slots):
            block = coup_mat[source * slots + j]
            pieces = []
            if j > 0:
                pieces.append(jnp.zeros((rank, j * rank), F32))
            pieces.append(block)
            if j < slots - 1:
                pieces.append(jnp.zeros((rank, (slots - 1 - j) * rank), F32))
            high, low = split(jnp.concatenate(pieces, axis=1))
            far_high[source, j * rank : (j + 1) * rank] = high
            far_low[source, j * rank : (j + 1) * rank] = low

    over(members, one)

    nothing = jnp.zeros((members // 4, LANES, LANES), BF16)
    far_high[members:] = nothing
    far_low[members:] = nothing
    blank = jnp.zeros((rank, LANES - rank), F32)

    def place(group, value):
        high, low = split(value)
        far_high[members + group, 2 * rank : 3 * rank] = high
        far_low[members + group, 2 * rank : 3 * rank] = low

    own = jnp.zeros((rank, LANES), F32)
    path = None
    for j in range(height):
        number = members >> j
        node = position >> j
        if j > 0:
            mixer = members - (members >> (j - 1)) + node
            step = upper_trans[mixer * 2 + ((position >> (j - 1)) & 1)]
            path = step if path is None else product(step, path, contract_nn)
        coupler = upper_coup[2 * members - 2 * number + node]
        start = coupler if path is None else product(path, coupler, contract_tn)
        current = [(node ^ 1, start)]
        for lower in range(j, 0, -1):
            offset = members - (members >> (lower - 1))
            following = []
            for index, matrix in current:
                for c in range(2):
                    mixed = product(matrix, upper_trans[(offset + index) * 2 + c], contract_nn)
                    following.append((2 * index + c, mixed))
            current = following
        if j < 2:
            for index, matrix in current:
                wide = jnp.concatenate([matrix, blank], axis=1)
                own = own + pltpu.roll(wide, (index & 3) * rank, 1)
        else:
            for k in range(0, len(current), 4):
                wide = jnp.concatenate([matrix for _, matrix in current[k : k + 4]], axis=1)
                place(current[k][0] >> 2, wide)
    place(position >> 2, own)


def near_kernel(
    vec_far,
    sub_half,
    cross_half,
    near_mat_far,
    near_src_far,
    near_count_far,
    near,
    vec,
    near_mat,
    near_src,
    near_count,
    values,
    semaphores,
    block_semaphores,
):
    arriving = fetch((vec_far, near_src_far, near_count_far), (vec, near_src, near_count), semaphores)
    chunks = block_semaphores.shape[0]
    chunk = near_mat.shape[0] // chunks

    def chunk_copy(k):
        rows = pl.ds(k * chunk, chunk)
        return pltpu.make_async_copy(near_mat_far.at[rows], near_mat.at[rows], block_semaphores.at[k])

    for k in range(chunks):
        chunk_copy(k).start()
    position = lax.axis_index(BRANCH)
    for copy in arriving:
        copy.wait()
    leaf_dev, slots, leaf_size, _ = near_mat.shape
    vecs = vec.shape[0]
    even = position % 2 == 0
    halo = leaf_dev // 2
    left = lane_part(vecs, leaf_size) == 0

    def lay(base, block):
        for m in range(block.shape[1] // LANES):
            pair = block[:, m * LANES : (m + 1) * LANES]
            swapped = pltpu.roll(pair, leaf_size, 1)
            for c, twice in enumerate((jnp.where(left, pair, swapped), jnp.where(left, swapped, pair))):
                high, low = split(twice)
                values[base + 2 * m + c, :vecs] = high
                values[base + 2 * m + c, vecs:] = low

    lay(halo, vec[...])
    lay(0, jnp.where(even, cross_half[...], sub_half[...]))
    lay(halo + leaf_dev, jnp.where(even, sub_half[...], cross_half[...]))
    values[2 * leaf_dev] = jnp.zeros((2 * vecs, LANES), BF16)
    shift = halo - position * leaf_dev
    wide_left = lane_part(2 * vecs, leaf_size) == 0
    out_left = lane_part(vecs, leaf_size) == 0

    def source(leaf, slot):
        live = slot < near_count[0, leaf]
        return values[jnp.where(live, near_src[slot, leaf] + shift, 2 * leaf_dev)]

    def two_leaves(pair):
        total = None
        leaves = (2 * pair, 2 * pair + 1)
        for tile in range(0, slots, 4):
            columns = min(4, slots - tile)
            rows_x = []
            rows_w = []
            for leaf in leaves:
                xs = []
                ws = []
                for i in range(tile, tile + columns, 2):
                    if i + 1 < tile + columns:
                        xs.append(jnp.where(wide_left, source(leaf, i), source(leaf, i + 1)))
                        ws.append(jnp.concatenate([near_mat[leaf, i], near_mat[leaf, i + 1]], axis=1))
                    else:
                        xs.append(source(leaf, i))
                        blank = jnp.zeros((leaf_size, LANES - leaf_size), F32)
                        ws.append(jnp.concatenate([near_mat[leaf, i], blank], axis=1))
                rows_x.append(jnp.concatenate(xs, axis=1) if len(xs) > 1 else xs[0])
                rows_w.append(jnp.concatenate(ws, axis=1) if len(ws) > 1 else ws[0])
            x = jnp.concatenate(rows_x, axis=0)
            high, low = split(jnp.concatenate(rows_w, axis=0))
            term = contract_nt(x, high) + contract_nt(x, low)
            total = term if total is None else total + term
        first = total[:vecs] + total[vecs : 2 * vecs]
        second = total[2 * vecs : 3 * vecs] + total[3 * vecs :]
        lanes = pl.ds(pl.multiple_of(pair * LANES, LANES), LANES)
        near[:, lanes] = jnp.where(out_left, first, second)

    def body(k, carry):
        chunk_copy(k).wait()
        for m in range(chunk // 2):
            two_leaves(k * (chunk // 2) + m)
        return carry

    lax.fori_loop(0, chunks, body, 0)


def down_kernel(
    members,
    slots,
    incoming,
    far_high,
    far_low,
    weights,
    near,
    coup_tgt_far,
    out,
    coup_tgt,
    far,
    semaphores,
):
    arriving = fetch((coup_tgt_far,), (coup_tgt,), semaphores)
    basis_high, basis_low, trans_high, trans_low = (weights.at[i] for i in range(4))
    vecs = out.shape[0]
    rank = LANES // slots
    groups = far.shape[0]
    far[...] = jnp.zeros(far.shape, F32)
    part = lane_part(vecs, rank)
    arriving[0].wait()

    def scatter(source):
        piece = times(incoming[source, :vecs], far_high[source], far_low[source], contract_nt)
        for j in range(slots):
            node = coup_tgt[j, source]
            alone = jnp.where(part == j, piece, 0.0)
            far[node >> 2] += pltpu.roll(alone, ((node - j) & 3) * rank, 1)

    over(members, scatter)

    few = lane_part(vecs // 2, rank)
    term = jnp.zeros((vecs, LANES), F32)
    for g in range(members // 4):
        first = jnp.zeros((vecs // 2, LANES), F32)
        second = jnp.zeros((vecs // 2, LANES), F32)
        for q in range(4):
            rows = incoming[4 * g + q, vecs:]
            first = jnp.where(few == q, rows, first)
            second = jnp.where(few == (q + 1) % 4, rows, second)
        tops = jnp.concatenate([first, pltpu.roll(second, LANES - rank, 1)], axis=0)
        term = term + times(tops, far_high[members + g], far_low[members + g], contract_nt)

    last = groups - 1
    weight = trans_high.shape[0] - 1
    base = far[last] + term
    two = base + times(base, trans_high[weight, :, LANES:], trans_low[weight, :, LANES:], contract_nn)
    first = last - 1
    level = [far[first] + times(two, trans_high[weight, :, :LANES], trans_low[weight, :, :LANES], contract_nn)]
    while first > 0:
        first -= 2 * len(level)
        weight -= len(level)
        children = []
        for g, value in enumerate(level):
            spread = times(value, trans_high[weight + g], trans_low[weight + g], contract_nn)
            children.append(far[first + 2 * g] + spread[:, :LANES])
            children.append(far[first + 2 * g + 1] + spread[:, LANES:])
        level = children
    for g, value in enumerate(level):
        lanes = slice(2 * LANES * g, 2 * LANES * (g + 1))
        out[:, lanes] = near[:, lanes] + times(value, basis_high[g], basis_low[g], contract_nn)


def in_hbm(x):
    return pltpu.with_memory_space_constraint(x, pltpu.HBM)


HBM_SPEC = pl.BlockSpec(memory_space=pltpu.HBM)
VMEM_SPEC = pl.BlockSpec(memory_space=pltpu.VMEM)


def params(mib):
    return pltpu.CompilerParams(vmem_limit_bytes=mib * MIB)


def cost(flops, size):
    return pl.CostEstimate(flops=flops, bytes_accessed=size, transcendentals=0)


def body(
    vectors,
    basis,
    trans,
    upper_trans,
    upper_coup,
    send_node,
    send_count,
    coup_tgt,
    coup_mat,
    near_src,
    near_count,
    near_mat,
):
    vecs, points = vectors.shape
    leaf_dev, rank, leaf_size = basis.shape
    members = lax.axis_size(BRANCH)
    slots = send_node.shape[2]
    groups = leaf_dev // 4
    node_groups = 2 * groups
    trans_blocks = trans.reshape(-1, rank, rank)
    coup_blocks = coup_mat.reshape(-1, rank, rank)
    upper_blocks = upper_trans.reshape(-1, rank, rank)
    near_chunks = leaf_dev // 4
    shape = jax.ShapeDtypeStruct

    def held(*dims):
        return shape(dims, BF16)

    outgoing, sub_half, cross_half, weights = pl.pallas_call(
        functools.partial(up_kernel, members, slots),
        out_shape=[
            shape((members, vecs + vecs // 2, LANES), F32),
            shape((vecs, points // 2), F32),
            shape((vecs, points // 2), F32),
            held(4, groups, LANES, 2 * LANES),
        ],
        in_specs=[HBM_SPEC] * 5,
        out_specs=[VMEM_SPEC] * 4,
        scratch_shapes=[
            pltpu.VMEM((vecs, points), F32),
            pltpu.VMEM(basis.shape, F32),
            pltpu.VMEM(trans_blocks.shape, F32),
            pltpu.SMEM((slots, members), jnp.int32),
            pltpu.SMEM((1, members), jnp.int32),
            pltpu.VMEM((4 * node_groups + 8, vecs, LANES), F32),
            pltpu.SemaphoreType.DMA((5,)),
        ],
        compiler_params=params(8 + members // 4),
        name="up",
    )(
        in_hbm(vectors),
        in_hbm(basis),
        in_hbm(trans_blocks),
        in_hbm(jnp.transpose(send_node[0])),
        in_hbm(send_count),
    )
    incoming = lax.all_to_all(outgoing, BRANCH, split_axis=0, concat_axis=0, tiled=True)
    pairs = [(i, i ^ 1) for i in range(members)]
    sub_got = lax.ppermute(sub_half, BRANCH, pairs)
    pairs = [(i, i + 1) for i in range(1, members - 1, 2)]
    pairs = pairs + [(b, a) for a, b in pairs]
    cross_got = lax.ppermute(cross_half, BRANCH, pairs)

    far_high, far_low = pl.pallas_call(
        functools.partial(prepare_kernel, members, slots),
        out_shape=[
            held(members + members // 4, LANES, LANES),
            held(members + members // 4, LANES, LANES),
        ],
        in_specs=[HBM_SPEC] * 3,
        out_specs=[VMEM_SPEC] * 2,
        scratch_shapes=[
            pltpu.VMEM(coup_blocks.shape, F32),
            pltpu.VMEM(upper_blocks.shape, F32),
            pltpu.VMEM(upper_coup.shape, F32),
            pltpu.SemaphoreType.DMA((3,)),
        ],
        compiler_params=params(8 + members // 4),
        cost_estimate=cost(1 << 20, 4 << 20),
        name="prepare",
    )(
        in_hbm(coup_blocks),
        in_hbm(upper_blocks),
        in_hbm(upper_coup),
    )

    near = pl.pallas_call(
        near_kernel,
        out_shape=shape((vecs, points), F32),
        in_specs=[HBM_SPEC, VMEM_SPEC, VMEM_SPEC, HBM_SPEC, HBM_SPEC, HBM_SPEC],
        out_specs=VMEM_SPEC,
        scratch_shapes=[
            pltpu.VMEM((vecs, points), F32),
            pltpu.VMEM(near_mat.shape, F32),
            pltpu.SMEM(near_src.shape[::-1], jnp.int32),
            pltpu.SMEM((1, leaf_dev), jnp.int32),
            pltpu.VMEM((2 * leaf_dev + 1, 2 * vecs, LANES), BF16),
            pltpu.SemaphoreType.DMA((3,)),
            pltpu.SemaphoreType.DMA((near_chunks,)),
        ],
        compiler_params=params(16),
        cost_estimate=cost(1 << 28, 10 << 20),
        name="near",
    )(
        in_hbm(vectors),
        sub_got,
        cross_got,
        in_hbm(near_mat),
        in_hbm(jnp.transpose(near_src)),
        in_hbm(near_count.reshape(1, -1)),
    )

    return pl.pallas_call(
        functools.partial(down_kernel, members, slots),
        out_shape=shape((vecs, points), F32),
        in_specs=[VMEM_SPEC] * 5 + [HBM_SPEC],
        out_specs=VMEM_SPEC,
        scratch_shapes=[
            pltpu.SMEM((slots, members), jnp.int32),
            pltpu.VMEM((node_groups, vecs, LANES), F32),
            pltpu.SemaphoreType.DMA((1,)),
        ],
        compiler_params=params(8 + members // 4),
        name="down",
    )(
        incoming,
        far_high,
        far_low,
        weights,
        near,
        in_hbm(jnp.transpose(coup_tgt[0])),
    )


def solution(mesh):
    spread = ("parts",) + BRANCH
    return jax.shard_map(
        body,
        mesh=mesh,
        in_specs=(
            P(None, spread),
            P(spread, None, None),
            P(spread, None, None, None, None),
            P("parts", None, None, None),
            P("parts", None, None),
            P(spread, None, None),
            P(spread, None),
            P(spread, None, None),
            P(spread, None, None, None, None),
            P(spread, None),
            P(spread),
            P(spread, None, None, None),
        ),
        out_specs=P(None, spread),
        check_vma=False,
    )
```

time: 79.1 us -> 29.5 us (0.37)
  the two profiles are of different devices: /device:TPU:0 before, /device:TPU:1 now
where the time goes in v1:
time: 29.5 us; the launch traced here: 29.2 us
  Pallas kernels  16.2 us (55%)
  starting transfers between devices  11 us (37%)
  local copies, waits for them, and re-layouts  1.91 us (6%)
    all_to_all x1, starting transfers between devices, body(): lax.all_to_all(outgoing, BRANCH, split_axis=0, concat_axis=0, tiled=True)  7.33 us
    pallas_call x1, Pallas kernels, body(): pl.pallas_call(near_kernel, out_shape=shape((vecs, points), F32), in_spec...  6.34 us
    pallas_call x1, Pallas kernels, body(): pl.pallas_call(functools.partial(up_kernel, members, slots), out_shape=[s...  3.63 us
    ppermute x1, starting transfers between devices, body(): cross_got = lax.ppermute(cross_half, BRANCH, pairs)  3.51 us
    pallas_call x1, Pallas kernels, body(): pl.pallas_call(functools.partial(prepare_kernel, members, slots), out_sha...  3.16 us
    pallas_call x1, Pallas kernels, body(): pl.pallas_call(functools.partial(down_kernel, members, slots), out_shape=...  3.07 us
    unnamed x4, local copies, waits for them, and re-layouts  1.91 us
  transfers between devices with their start and end apart: 3, of which 0 were waited for; matrix products, arithmetic and copies ran while one was open for 0% of the time, Pallas kernels for 33%

profile of v1, /device:TPU:1, one launch (start us, length us, event | category | flops | bytes accessed | tf_op | source)
XLA Modules:
  0.0 29.2 jit_solution(13110676476450138526)
XLA Ops:
  0.0 3.6 %up.1 = (f32[16,24,128]{2,1,0:T(8,128)}, f32[16,1024]{1,0:T(8,128)S(1)}, f32[16,1024]{1,0:T(8,128)S(1)}, bf16[4,8,128,256]{3,2,1,0:T(8,128)(2,1)S(1)}) custom-call(f32[16,2048]{1,0:T(8,128)} %vec_far.3, f32[32,32,64]{2,1,0:T(8,128)} %basis_far.1, f32[62,32,32]{2,1,0:T(8,128)} %bitcast.12, s32[4,16]{1,0:T(4,128)} %bitcast.16, s32[1,16]{1,0:T(1,128)} %send_count_far.1), custom_call_target="tpu_custom_call" | custom-call | tf_op jit(solution)/shard_map/up/pallas_call | solution.py:475
  3.6 7.3 %all-to-all-start = ((f32[16,24,128]{2,1,0:T(8,128)}), f32[16,24,128]{2,1,0:T(8,128)S(1)}, u32[]{:S(2)}, u32[]{:S(2)}) async-start(f32[16,24,128]{2,1,0:T(8,128)} %get-tuple-element.11), calls=%async_computation | async-start | bytes 393216 | tf_op jit(solution)/shard_map/all_to_all | solution.py:503
  11.0 0.2 collective-permute-start
  11.1 3.5 %collective-permute-start.1 = (f32[16,1024]{1,0:T(8,128)S(1)}, f32[16,1024]{1,0:T(8,128)S(1)}, u32[]{:S(2)}, u32[]{:S(2)}) collective-permute-start(f32[16,1024]{1,0:T(8,128)S(1)} %get-tuple-element.16), channel_id=1, source_target_pairs={{1,2},{3,4},{5,6},{7,8},{9,10},{11,12},{13,14},{2,1},{4,3},{6,5},{... | collective-permute-start | bytes 196616 | tf_op jit(solution)/shard_map/ppermute | solution.py:508
  14.7 3.2 %prepare.1 = (bf16[20,128,128]{2,1,0:T(8,128)(2,1)S(1)}, bf16[20,128,128]{2,1,0:T(8,128)(2,1)S(1)}) custom-call(f32[64,32,32]{2,1,0:T(8,128)} %bitcast.11, f32[30,32,32]{2,1,0:T(8,128)} %bitcast.13, f32[30,32,32]{2,1,0:T(8,128)} %upper_coup_far.1), custom_call_target="tpu_custom_call" | custom-call | flops 1048576 | bytes 4194304 | tf_op jit(solution)/shard_map/prepare/pallas_call | solution.py:510
  17.8 0.0 copy-start
  17.8 0.8 %copy-done = bf16[20,128,128]{2,1,0:T(8,128)(2,1)} copy-done((bf16[20,128,128]{2,1,0:T(8,128)(2,1)}, bf16[20,128,128]{2,1,0:T(8,128)(2,1)S(1)}, u32[]{:S(2)}) %copy-start) | copy-done | bytes 655384
  18.7 0.0 collective-permute-done.sub_half
  18.7 0.0 collective-permute-done.1.cross_half
  18.7 6.3 %near.1 = f32[16,2048]{1,0:T(8,128)S(1)} custom-call(f32[16,2048]{1,0:T(8,128)} %vec_far.3, f32[16,1024]{1,0:T(8,128)S(1)} %collective-permute-done.sub_half, f32[16,1024]{1,0:T(8,128)S(1)} %collective-permute-done.1.cross_half, f32[32,9,64,64]{3,2,1,0:T(8,128)} %near_mat_far.1, s32[9,32]{1,0:T(8,128)} %bitcast.14, s32[1,32]{1,0:T(1,128)} %bitcast.17), custom_call_target="tpu_custom_call" | custom-call | flops 268435456 | bytes 10485760 | tf_op jit(solution)/shard_map/near/pallas_call | solution.py:533
  25.0 0.0 all-to-all-done.incoming
  25.0 0.0 copy-start.1
  25.0 1.1 %copy-done.1 = bf16[20,128,128]{2,1,0:T(8,128)(2,1)S(1)} copy-done((bf16[20,128,128]{2,1,0:T(8,128)(2,1)S(1)}, bf16[20,128,128]{2,1,0:T(8,128)(2,1)}, u32[]{:S(2)}) %copy-start.1) | copy-done | bytes 655384
  26.1 3.1 %down.1 = f32[16,2048]{1,0:T(8,128)} custom-call(f32[16,24,128]{2,1,0:T(8,128)S(1)} %all-to-all-done.incoming, bf16[20,128,128]{2,1,0:T(8,128)(2,1)S(1)} %get-tuple-element.12.far_high, bf16[20,128,128]{2,1,0:T(8,128)(2,1)S(1)} %copy-done.1, bf16[4,8,128,256]{3,2,1,0:T(8,128)(2,1)S(1)} %get-tuple-element.14.weights, f32[16,2048]{1,0:T(8,128)S(1)} %near.1, ...), custom_call_target="tpu_custom_call" | custom-call | tf_op jit(solution)/shard_map/down/pallas_call | solution.py:559
Async XLA Ops:
  3.6 21.4 %all-to-all-start = ((f32[16,24,128]{2,1,0:T(8,128)}), f32[16,24,128]{2,1,0:T(8,128)S(1)}, u32[]{:S(2)}, u32[]{:S(2)}) async-start(f32[16,24,128]{2,1,0:T(8,128)} %get-tuple-element.11), calls=%async_computation | async-start | bytes 393216 | tf_op jit(solution)/shard_map/all_to_all | solution.py:503
  11.0 7.7 %collective-permute-start = (f32[16,1024]{1,0:T(8,128)S(1)}, f32[16,1024]{1,0:T(8,128)S(1)}, u32[]{:S(2)}, u32[]{:S(2)}) collective-permute-start(f32[16,1024]{1,0:T(8,128)S(1)} %get-tuple-element.15), channel_id=1, source_target_pairs={{0,1},{1,0},{2,3},{3,2},{4,5},{5,4},{6,7},{7,6},{8,9},{9,8},{10,11... | collective-permute-start | bytes 196616 | tf_op jit(solution)/shard_map/ppermute | solution.py:505
  11.1 7.5 %collective-permute-start.1 = (f32[16,1024]{1,0:T(8,128)S(1)}, f32[16,1024]{1,0:T(8,128)S(1)}, u32[]{:S(2)}, u32[]{:S(2)}) collective-permute-start(f32[16,1024]{1,0:T(8,128)S(1)} %get-tuple-element.16), channel_id=1, source_target_pairs={{1,2},{3,4},{5,6},{7,8},{9,10},{11,12},{13,14},{2,1},{4,3},{6,5},{... | collective-permute-start | bytes 196616 | tf_op jit(solution)/shard_map/ppermute | solution.py:508
  17.8 0.8 %copy-start = (bf16[20,128,128]{2,1,0:T(8,128)(2,1)}, bf16[20,128,128]{2,1,0:T(8,128)(2,1)S(1)}, u32[]{:S(2)}) copy-start(bf16[20,128,128]{2,1,0:T(8,128)(2,1)S(1)} %get-tuple-element.13.far_low) | copy-start | bytes 1966084
  25.0 1.1 %copy-start.1 = (bf16[20,128,128]{2,1,0:T(8,128)(2,1)S(1)}, bf16[20,128,128]{2,1,0:T(8,128)(2,1)}, u32[]{:S(2)}) copy-start(bf16[20,128,128]{2,1,0:T(8,128)(2,1)} %copy-done) | copy-start | bytes 1966084

commit v2 on v1

--- a/solution.py
+++ b/solution.py
@@ -91,77 +91,66 @@
     rolled,
     semaphores,
 ):
+    position = lax.axis_index(BRANCH)
+    half = vec.shape[1] // 2
+    start = (position & 1) * half
+    at_partner = vec_far.at[:, pl.ds(pl.multiple_of(half - start, LANES), half)]
+    at_neighbour = vec_far.at[:, pl.ds(pl.multiple_of(start, LANES), half)]
     arriving = fetch(
-        (vec_far, basis_far, trans_far, send_node_far, send_count_far),
-        (vec, basis, trans, send_node, send_count),
+        (vec_far, basis_far, trans_far, send_node_far, send_count_far, at_partner, at_neighbour),
+        (vec, basis, trans, send_node, send_count, sub_half, cross_half),
         semaphores,
     )
     basis_high, basis_low, trans_high, trans_low = (weights.at[i] for i in range(4))
-    position = lax.axis_index(BRANCH)
     leaf_dev, rank, leaf_size = basis.shape
     vecs = vec.shape[0]
+    left = lane_part(vecs, LANES // 2) == 0
+    blank = jnp.zeros((rank, LANES // 2), F32)
+
     arriving[0].wait()
     arriving[1].wait()
-    half = vec.shape[1] // 2
-    even = position % 2 == 0
-    low_half = vec[:, :half]
-    high_half = vec[:, half:]
-    sub_half[...] = jnp.where(even, high_half, low_half)
-    cross_half[...] = jnp.where(even, low_half, high_half)
-
     for leaf in range(leaf_dev):
         group, q = leaf // 4, leaf % 4
-        blank = jnp.zeros((rank, LANES - leaf_size), F32)
-        pieces = [basis[leaf], blank] if q % 2 == 0 else [blank, basis[leaf]]
-        high, low = split(jnp.concatenate(pieces, axis=1))
-        rows = slice(q * rank, (q + 1) * rank)
-        here = slice(0, LANES) if q < 2 else slice(LANES, 2 * LANES)
-        other = slice(LANES, 2 * LANES) if q < 2 else slice(0, LANES)
-        basis_high[group, rows, here] = high
-        basis_low[group, rows, here] = low
-        basis_high[group, rows, other] = jnp.zeros((rank, LANES), BF16)
-        basis_low[group, rows, other] = jnp.zeros((rank, LANES), BF16)
+        high, low = split(jnp.concatenate([basis[leaf], blank] if q % 2 == 0 else [blank, basis[leaf]], axis=1))
+        basis_high[group, q * rank : (q + 1) * rank] = high
+        basis_low[group, q * rank : (q + 1) * rank] = low
+    def keep(group, value):
+        for k in range(4):
+            rolled[4 * group + k] = value if k == 0 else pltpu.roll(value, k * rank, 1)
+
+    def joined(first, second, high, low):
+        both = times(jnp.concatenate([first, second], axis=0), high, low, contract_nt)
+        return jnp.where(left, both[:vecs], both[vecs:])
+
+    level = []
+    for g in range(leaf_dev // 4):
+        first = vec[:, 2 * LANES * g : 2 * LANES * g + LANES]
+        second = vec[:, 2 * LANES * g + LANES : 2 * LANES * (g + 1)]
+        level.append(joined(first, second, basis_high[g], basis_low[g]))
+        keep(g, level[g])
     arriving[2].wait()
     for node in range(leaf_dev):
         group, q = node // 4, node % 4
-        rows = slice(q * rank, (q + 1) * rank)
-        here = slice(0, LANES) if q < 2 else slice(LANES, 2 * LANES)
-        other = slice(LANES, 2 * LANES) if q < 2 else slice(0, LANES)
         if node < leaf_dev - 1:
             pair = [trans[2 * node], trans[2 * node + 1]]
-            blank = jnp.zeros((rank, LANES - 2 * rank), F32)
-            pieces = pair + [blank] if q % 2 == 0 else [blank] + pair
-            high, low = split(jnp.concatenate(pieces, axis=1))
+            high, low = split(jnp.concatenate(pair + [blank] if q % 2 == 0 else [blank] + pair, axis=1))
         else:
             high = low = jnp.zeros((rank, LANES), BF16)
-        trans_high[group, rows, here] = high
-        trans_low[group, rows, here] = low
-        trans_high[group, rows, other] = jnp.zeros((rank, LANES), BF16)
-        trans_low[group, rows, other] = jnp.zeros((rank, LANES), BF16)
-
-    def keep(group, value):
-        for k in range(4):
-            rolled[4 * group + k] = value if k == 0 else pltpu.roll(value, k * rank, 1)
-
-    level = []
-    for g in range(leaf_dev // 4):
-        x = vec[:, 2 * LANES * g : 2 * LANES * (g + 1)]
-        level.append(times(x, basis_high[g], basis_low[g], contract_nt))
-        keep(g, level[g])
+        trans_high[group, q * rank : (q + 1) * rank] = high
+        trans_low[group, q * rank : (q + 1) * rank] = low
     done = leaf_dev // 4
     weight = 0
     while len(level) > 1:
         nodes = []
         for g in range(len(level) // 2):
-            children = jnp.concatenate([level[2 * g], level[2 * g + 1]], axis=1)
-            nodes.append(times(children, trans_high[weight], trans_low[weight], contract_nt))
+            nodes.append(joined(level[2 * g], level[2 * g + 1], trans_high[weight], trans_low[weight]))
             keep(done, nodes[g])
             weight += 1
             done += 1
         level = nodes
-    two = times(level[0], trans_high[weight, :, :LANES], trans_low[weight, :, :LANES], contract_nt)
-    top = times(two, trans_high[weight, :, LANES:], trans_low[weight, :, LANES:], contract_nt)
-    keep(done, two + top)
+    two = jnp.where(left, times(level[0], trans_high[weight], trans_low[weight], contract_nt), 0.0)
+    top = times(two, trans_high[weight], trans_low[weight], contract_nt)
+    keep(done, jnp.where(left, two, top))
     blank_index = 4 * (done + 1)
     rolled[blank_index] = jnp.zeros((vecs, LANES), F32)
 
@@ -189,37 +178,20 @@
         outgoing[target, vecs:] = top_rows
 
     over(members, pick)
-
-
-def prepare_kernel(
-    members,
-    slots,
-    coup_mat_far,
-    upper_trans_far,
-    upper_coup_far,
-    far_high,
-    far_low,
-    coup_mat,
-    upper_trans,
-    upper_coup,
-    semaphores,
-):
-    arriving = fetch(
-        (coup_mat_far, upper_trans_far, upper_coup_far), (coup_mat, upper_trans, upper_coup), semaphores
-    )
+    arriving[5].wait()
+    arriving[6].wait()
+
+
+def prepare(members, slots, coup_mat, upper_trans, upper_coup, far_high, far_low):
     position = lax.axis_index(BRANCH)
-    for copy in arriving:
-        copy.wait()
     rank = coup_mat.shape[1]
     height = members.bit_length() - 1
 
     def one(source):
         for j in range(slots):
-            block = coup_mat[source * slots + j]
-            pieces = []
+            pieces = [coup_mat[source * slots + j]]
             if j > 0:
-                pieces.append(jnp.zeros((rank, j * rank), F32))
-            pieces.append(block)
+                pieces.insert(0, jnp.zeros((rank, j * rank), F32))
             if j < slots - 1:
                 pieces.append(jnp.zeros((rank, (slots - 1 - j) * rank), F32))
             high, low = split(jnp.concatenate(pieces, axis=1))
@@ -269,39 +241,45 @@
     place(position >> 2, own)
 
 
-def near_kernel(
+def near_half(
+    first,
+    halo_half,
     vec_far,
-    sub_half,
-    cross_half,
-    near_mat_far,
     near_src_far,
     near_count_far,
+    near_mat_far,
     near,
     vec,
-    near_mat,
     near_src,
     near_count,
+    near_mat,
     values,
     semaphores,
     block_semaphores,
+    before,
 ):
+    position = lax.axis_index(BRANCH)
+    leaves, near_slots, leaf_size, _ = near_mat.shape
+    leaf_dev = 2 * leaves
+    vecs = vec.shape[0]
+    halo = leaf_dev // 2
+    upper = (position & 1) ^ (1 if first else 0)
+    base = upper * leaves
     arriving = fetch((vec_far, near_src_far, near_count_far), (vec, near_src, near_count), semaphores)
     chunks = block_semaphores.shape[0]
-    chunk = near_mat.shape[0] // chunks
+    chunk = leaves // chunks
 
     def chunk_copy(k):
-        rows = pl.ds(k * chunk, chunk)
-        return pltpu.make_async_copy(near_mat_far.at[rows], near_mat.at[rows], block_semaphores.at[k])
+        here = pl.ds(k * chunk, chunk)
+        return pltpu.make_async_copy(
+            near_mat_far.at[pl.ds(base + k * chunk, chunk)], near_mat.at[here], block_semaphores.at[k]
+        )
 
     for k in range(chunks):
         chunk_copy(k).start()
-    position = lax.axis_index(BRANCH)
+    before()
     for copy in arriving:
         copy.wait()
-    leaf_dev, slots, leaf_size, _ = near_mat.shape
-    vecs = vec.shape[0]
-    even = position % 2 == 0
-    halo = leaf_dev // 2
     left = lane_part(vecs, leaf_size) == 0
 
     def lay(base, block):
@@ -313,23 +291,21 @@
                 values[base + 2 * m + c, :vecs] = high
                 values[base + 2 * m + c, vecs:] = low
 
+    lay(upper * (halo + leaf_dev), halo_half[...])
     lay(halo, vec[...])
-    lay(0, jnp.where(even, cross_half[...], sub_half[...]))
-    lay(halo + leaf_dev, jnp.where(even, sub_half[...], cross_half[...]))
     values[2 * leaf_dev] = jnp.zeros((2 * vecs, LANES), BF16)
     shift = halo - position * leaf_dev
     wide_left = lane_part(2 * vecs, leaf_size) == 0
-    out_left = lane_part(vecs, leaf_size) == 0
 
     def source(leaf, slot):
-        live = slot < near_count[0, leaf]
-        return values[jnp.where(live, near_src[slot, leaf] + shift, 2 * leaf_dev)]
+        live = slot < near_count[0, base + leaf]
+        return values[jnp.where(live, near_src[slot, base + leaf] + shift, 2 * leaf_dev)]
 
     def two_leaves(pair):
         total = None
         leaves = (2 * pair, 2 * pair + 1)
-        for tile in range(0, slots, 4):
-            columns = min(4, slots - tile)
+        for tile in range(0, near_slots, 4):
+            columns = min(4, near_slots - tile)
             rows_x = []
             rows_w = []
             for leaf in leaves:
@@ -351,16 +327,52 @@
             total = term if total is None else total + term
         first = total[:vecs] + total[vecs : 2 * vecs]
         second = total[2 * vecs : 3 * vecs] + total[3 * vecs :]
-        lanes = pl.ds(pl.multiple_of(pair * LANES, LANES), LANES)
-        near[:, lanes] = jnp.where(out_left, first, second)
-
-    def body(k, carry):
+        lanes = pl.ds(pl.multiple_of((base // 2 + pair) * LANES, LANES), LANES)
+        near[:, lanes] = jnp.where(left, first, second)
+
+    for k in range(chunks):
         chunk_copy(k).wait()
         for m in range(chunk // 2):
             two_leaves(k * (chunk // 2) + m)
-        return carry
-
-    lax.fori_loop(0, chunks, body, 0)
+
+
+def first_kernel(
+    members,
+    slots,
+    halo_half,
+    vec_far,
+    near_src_far,
+    near_count_far,
+    near_mat_far,
+    coup_mat_far,
+    upper_trans_far,
+    upper_coup_far,
+    near,
+    far_high,
+    far_low,
+    coup_mat,
+    upper_trans,
+    upper_coup,
+    prepare_semaphores,
+    *scratch,
+):
+    arriving = fetch(
+        (upper_trans_far, upper_coup_far, coup_mat_far), (upper_trans, upper_coup, coup_mat), prepare_semaphores
+    )
+
+    def before():
+        for copy in arriving:
+            copy.wait()
+        prepare(members, slots, coup_mat, upper_trans, upper_coup, far_high, far_low)
+
+    near_half(True, halo_half, vec_far, near_src_far, near_count_far, near_mat_far, near, *scratch, before)
+
+
+def second_kernel(halo_half, vec_far, near_src_far, near_count_far, near_mat_far, near_first, near, *scratch):
+    del near_first
+    near_half(
+        False, halo_half, vec_far, near_src_far, near_count_far, near_mat_far, near, *scratch, lambda: None
+    )
 
 
 def down_kernel(
@@ -375,6 +387,7 @@
     out,
     coup_tgt,
     far,
+    pieces,
     semaphores,
 ):
     arriving = fetch((coup_tgt_far,), (coup_tgt,), semaphores)
@@ -384,16 +397,11 @@
     groups = far.shape[0]
     far[...] = jnp.zeros(far.shape, F32)
     part = lane_part(vecs, rank)
-    arriving[0].wait()
-
-    def scatter(source):
-        piece = times(incoming[source, :vecs], far_high[source], far_low[source], contract_nt)
-        for j in range(slots):
-            node = coup_tgt[j, source]
-            alone = jnp.where(part == j, piece, 0.0)
-            far[node >> 2] += pltpu.roll(alone, ((node - j) & 3) * rank, 1)
-
-    over(members, scatter)
+
+    def couple(source):
+        pieces[source] = times(incoming[source, :vecs], far_high[source], far_low[source], contract_nt)
+
+    over(members, couple)
 
     few = lane_part(vecs // 2, rank)
     term = jnp.zeros((vecs, LANES), F32)
@@ -406,25 +414,48 @@
             second = jnp.where(few == (q + 1) % 4, rows, second)
         tops = jnp.concatenate([first, pltpu.roll(second, LANES - rank, 1)], axis=0)
         term = term + times(tops, far_high[members + g], far_low[members + g], contract_nt)
-
-    last = groups - 1
+    arriving[0].wait()
+
+    def scatter(source):
+        piece = pieces[source]
+        for j in range(slots):
+            node = coup_tgt[j, source]
+            alone = jnp.where(part == j, piece, 0.0)
+            far[node >> 2] += pltpu.roll(alone, ((node - j) & 3) * rank, 1)
+
+    over(members, scatter)
+
+    left = part < 2
     weight = trans_high.shape[0] - 1
-    base = far[last] + term
-    two = base + times(base, trans_high[weight, :, LANES:], trans_low[weight, :, LANES:], contract_nn)
-    first = last - 1
-    level = [far[first] + times(two, trans_high[weight, :, :LANES], trans_low[weight, :, :LANES], contract_nn)]
+
+    def first_half(x):
+        return jnp.where(left, x, 0.0)
+
+    def second_half(x):
+        return jnp.where(left, 0.0, x)
+
+    def spread(x, high, low):
+        both = times(jnp.concatenate([first_half(x), second_half(x)], axis=0), high, low, contract_nn)
+        return both[:vecs], both[vecs:]
+
+    first = groups - 2
+    high, low = trans_high[weight], trans_low[weight]
+    base = far[first + 1] + term
+    two = base + times(second_half(base), high, low, contract_nn)
+    level = [far[first] + times(first_half(two), high, low, contract_nn)]
     while first > 0:
         first -= 2 * len(level)
         weight -= len(level)
         children = []
         for g, value in enumerate(level):
-            spread = times(value, trans_high[weight + g], trans_low[weight + g], contract_nn)
-            children.append(far[first + 2 * g] + spread[:, :LANES])
-            children.append(far[first + 2 * g + 1] + spread[:, LANES:])
+            pair = spread(value, trans_high[weight + g], trans_low[weight + g])
+            children.append(far[first + 2 * g] + pair[0])
+            children.append(far[first + 2 * g + 1] + pair[1])
         level = children
     for g, value in enumerate(level):
-        lanes = slice(2 * LANES * g, 2 * LANES * (g + 1))
-        out[:, lanes] = near[:, lanes] + times(value, basis_high[g], basis_low[g], contract_nn)
+        for c, points in enumerate(spread(value, basis_high[g], basis_low[g])):
+            lanes = slice(LANES * (2 * g + c), LANES * (2 * g + c + 1))
+            out[:, lanes] = near[:, lanes] + points
 
 
 def in_hbm(x):
@@ -466,7 +497,7 @@
     trans_blocks = trans.reshape(-1, rank, rank)
     coup_blocks = coup_mat.reshape(-1, rank, rank)
     upper_blocks = upper_trans.reshape(-1, rank, rank)
-    near_chunks = leaf_dev // 4
+    near_chunks = leaf_dev // 16
     shape = jax.ShapeDtypeStruct
 
     def held(*dims):
@@ -478,7 +509,7 @@
             shape((members, vecs + vecs // 2, LANES), F32),
             shape((vecs, points // 2), F32),
             shape((vecs, points // 2), F32),
-            held(4, groups, LANES, 2 * LANES),
+            held(4, groups, LANES, LANES),
         ],
         in_specs=[HBM_SPEC] * 5,
         out_specs=[VMEM_SPEC] * 4,
@@ -489,7 +520,7 @@
             pltpu.SMEM((slots, members), jnp.int32),
             pltpu.SMEM((1, members), jnp.int32),
             pltpu.VMEM((4 * node_groups + 8, vecs, LANES), F32),
-            pltpu.SemaphoreType.DMA((5,)),
+            pltpu.SemaphoreType.DMA((7,)),
         ],
         compiler_params=params(8 + members // 4),
         name="up",
@@ -501,60 +532,56 @@
         in_hbm(send_count),
     )
     incoming = lax.all_to_all(outgoing, BRANCH, split_axis=0, concat_axis=0, tiled=True)
-    pairs = [(i, i ^ 1) for i in range(members)]
-    sub_got = lax.ppermute(sub_half, BRANCH, pairs)
+    sub_got = lax.ppermute(sub_half, BRANCH, [(i, i ^ 1) for i in range(members)])
     pairs = [(i, i + 1) for i in range(1, members - 1, 2)]
-    pairs = pairs + [(b, a) for a, b in pairs]
-    cross_got = lax.ppermute(cross_half, BRANCH, pairs)
-
-    far_high, far_low = pl.pallas_call(
-        functools.partial(prepare_kernel, members, slots),
+    cross_got = lax.ppermute(cross_half, BRANCH, pairs + [(b, a) for a, b in pairs])
+
+    near_scratch = [
+        pltpu.VMEM((vecs, points), F32),
+        pltpu.SMEM(near_src.shape[::-1], jnp.int32),
+        pltpu.SMEM((1, leaf_dev), jnp.int32),
+        pltpu.VMEM((leaf_dev // 2,) + near_mat.shape[1:], F32),
+        pltpu.VMEM((2 * leaf_dev + 1, 2 * vecs, LANES), BF16),
+        pltpu.SemaphoreType.DMA((3,)),
+        pltpu.SemaphoreType.DMA((near_chunks,)),
+    ]
+    near_inputs = (
+        in_hbm(vectors),
+        in_hbm(jnp.transpose(near_src)),
+        in_hbm(near_count.reshape(1, -1)),
+        in_hbm(near_mat),
+    )
+    near, far_high, far_low = pl.pallas_call(
+        functools.partial(first_kernel, members, slots),
         out_shape=[
+            shape((vecs, points), F32),
             held(members + members // 4, LANES, LANES),
             held(members + members // 4, LANES, LANES),
         ],
-        in_specs=[HBM_SPEC] * 3,
-        out_specs=[VMEM_SPEC] * 2,
+        in_specs=[VMEM_SPEC] + [HBM_SPEC] * 7,
+        out_specs=[VMEM_SPEC] * 3,
         scratch_shapes=[
             pltpu.VMEM(coup_blocks.shape, F32),
             pltpu.VMEM(upper_blocks.shape, F32),
             pltpu.VMEM(upper_coup.shape, F32),
             pltpu.SemaphoreType.DMA((3,)),
-        ],
-        compiler_params=params(8 + members // 4),
-        cost_estimate=cost(1 << 20, 4 << 20),
-        name="prepare",
-    )(
-        in_hbm(coup_blocks),
-        in_hbm(upper_blocks),
-        in_hbm(upper_coup),
-    )
-
+        ]
+        + near_scratch,
+        compiler_params=params(12 + members // 4),
+        cost_estimate=cost(1 << 28, 16 << 20),
+        name="near_first",
+    )(sub_got, *near_inputs, in_hbm(coup_blocks), in_hbm(upper_blocks), in_hbm(upper_coup))
     near = pl.pallas_call(
-        near_kernel,
+        second_kernel,
         out_shape=shape((vecs, points), F32),
-        in_specs=[HBM_SPEC, VMEM_SPEC, VMEM_SPEC, HBM_SPEC, HBM_SPEC, HBM_SPEC],
+        in_specs=[VMEM_SPEC] + [HBM_SPEC] * 4 + [VMEM_SPEC],
         out_specs=VMEM_SPEC,
-        scratch_shapes=[
-            pltpu.VMEM((vecs, points), F32),
-            pltpu.VMEM(near_mat.shape, F32),
-            pltpu.SMEM(near_src.shape[::-1], jnp.int32),
-            pltpu.SMEM((1, leaf_dev), jnp.int32),
-            pltpu.VMEM((2 * leaf_dev + 1, 2 * vecs, LANES), BF16),
-            pltpu.SemaphoreType.DMA((3,)),
-            pltpu.SemaphoreType.DMA((near_chunks,)),
-        ],
-        compiler_params=params(16),
-        cost_estimate=cost(1 << 28, 10 << 20),
-        name="near",
-    )(
-        in_hbm(vectors),
-        sub_got,
-        cross_got,
-        in_hbm(near_mat),
-        in_hbm(jnp.transpose(near_src)),
-        in_hbm(near_count.reshape(1, -1)),
-    )
+        scratch_shapes=near_scratch,
+        input_output_aliases={5: 0},
+        compiler_params=params(12),
+        cost_estimate=cost(1 << 28, 8 << 20),
+        name="near_second",
+    )(cross_got, *near_inputs, near)
 
     return pl.pallas_call(
         functools.partial(down_kernel, members, slots),
@@ -564,6 +591,7 @@
         scratch_shapes=[
             pltpu.SMEM((slots, members), jnp.int32),
             pltpu.VMEM((node_groups, vecs, LANES), F32),
+            pltpu.VMEM((members, vecs, LANES), F32),
             pltpu.SemaphoreType.DMA((1,)),
         ],
         compiler_params=params(8 + members // 4),

time: 29.5 us -> 26.2 us (0.89)
  local copies, waits for them, and re-layouts: 1.91 us -> 0 us
  Pallas kernels: 16.2 us -> 14.8 us
    unnamed x4 -> x0, local copies, waits for them, and re-layouts: 1.91 us -> none
    pallas_call x2, Pallas kernels: 9.5 us -> 7.93 us  [the longest x1 4.77 us: body(): pl.pallas_call(functools.partial(first_kernel, members, slots), out_shape...]
  transfers between devices with their start and end apart: 3 -> 3, of which waited for: 0 -> 0; matrix products, arithmetic and copies ran while one was open for 0% -> 0% of each run, Pallas kernels for 33% -> 31%
where the time goes in v2:
time: 26.2 us; the launch traced here: 25.9 us
  Pallas kernels  14.8 us (56%)
  starting transfers between devices  11 us (42%)
    all_to_all x1, starting transfers between devices, body(): lax.all_to_all(outgoing, BRANCH, split_axis=0, concat_axis=0, tiled=True)  7.33 us
    pallas_call x1, Pallas kernels, body(): pl.pallas_call(functools.partial(first_kernel, members, slots), out_shape...  4.77 us
    pallas_call x1, Pallas kernels, body(): pl.pallas_call(functools.partial(up_kernel, members, slots), out_shape=[s...  3.64 us
    ppermute x1, starting transfers between devices, body(): lax.ppermute(cross_half, BRANCH, pairs + [(b, a) for a, b in pairs])  3.51 us
    pallas_call x1, Pallas kernels, body(): pl.pallas_call(functools.partial(down_kernel, members, slots), out_shape=...  3.28 us
    pallas_call x1, Pallas kernels, body(): pl.pallas_call(second_kernel, out_shape=shape((vecs, points), F32), in_sp...  3.16 us
  transfers between devices with their start and end apart: 3, of which 0 were waited for; matrix products, arithmetic and copies ran while one was open for 0% of the time, Pallas kernels for 31%

profile of v2, /device:TPU:1, one launch (start us, length us, event | category | flops | bytes accessed | tf_op | source)
XLA Modules:
  0.0 25.9 jit_solution(5632901882283965834)
XLA Ops:
  0.0 3.6 %up.1 = (f32[16,24,128]{2,1,0:T(8,128)}, f32[16,1024]{1,0:T(8,128)S(1)}, f32[16,1024]{1,0:T(8,128)S(1)}, bf16[4,8,128,128]{3,2,1,0:T(8,128)(2,1)S(1)}) custom-call(f32[16,2048]{1,0:T(8,128)} %vec_far.5, f32[32,32,64]{2,1,0:T(8,128)} %basis_far.1, f32[62,32,32]{2,1,0:T(8,128)} %bitcast.12, s32[4,16]{1,0:T(4,128)} %bitcast.16, s32[1,16]{1,0:T(1,128)} %send_count_far.1), custom_call_target="tpu_custom_call" | custom-call | tf_op jit(solution)/shard_map/up/pallas_call | solution.py:506
  3.6 7.3 %all-to-all-start = ((f32[16,24,128]{2,1,0:T(8,128)}), f32[16,24,128]{2,1,0:T(8,128)S(1)}, u32[]{:S(2)}, u32[]{:S(2)}) async-start(f32[16,24,128]{2,1,0:T(8,128)} %get-tuple-element.12), calls=%async_computation | async-start | bytes 393216 | tf_op jit(solution)/shard_map/all_to_all | solution.py:534
  11.0 0.2 collective-permute-start
  11.1 3.5 %collective-permute-start.1 = (f32[16,1024]{1,0:T(8,128)S(1)}, f32[16,1024]{1,0:T(8,128)S(1)}, u32[]{:S(2)}, u32[]{:S(2)}) collective-permute-start(f32[16,1024]{1,0:T(8,128)S(1)} %get-tuple-element.17), channel_id=1, source_target_pairs={{1,2},{3,4},{5,6},{7,8},{9,10},{11,12},{13,14},{2,1},{4,3},{6,5},{... | collective-permute-start | bytes 196616 | tf_op jit(solution)/shard_map/ppermute | solution.py:537
  14.7 0.0 collective-permute-done.halo_half
  14.7 4.8 %near_first.1 = (f32[16,2048]{1,0:T(8,128)S(1)}, bf16[20,128,128]{2,1,0:T(8,128)(2,1)S(1)}, bf16[20,128,128]{2,1,0:T(8,128)(2,1)S(1)}) custom-call(f32[16,1024]{1,0:T(8,128)S(1)} %collective-permute-done.halo_half, f32[16,2048]{1,0:T(8,128)} %vec_far.5, s32[9,32]{1,0:T(8,128)} %bitcast.14, s32[1,32]{1,0:T(1,128)} %bitcast.18, ...), custom_call_target="tpu_custom_call" | custom-call | flops 268435456 | bytes 16777216 | tf_op jit(solution)/shard_map/near_first/pallas_call | solution.py:554
  19.5 0.0 collective-permute-done.1.halo_half
  19.5 3.2 %near_second.1.near = f32[16,2048]{1,0:T(8,128)S(1)} custom-call(f32[16,1024]{1,0:T(8,128)S(1)} %collective-permute-done.1.halo_half, f32[16,2048]{1,0:T(8,128)} %vec_far.5, s32[9,32]{1,0:T(8,128)} %bitcast.15, s32[1,32]{1,0:T(1,128)} %bitcast.19, f32[32,9,64,64]{3,2,1,0:T(8,128)} %near_mat_far.3, ...), custom_call_target="tpu_custom_call", output_to_operand_aliasing={{}: (5, {})} | custom-call | flops 268435456 | bytes 8388608 | tf_op jit(solution)/shard_map/near_second/pallas_call | solution.py:574
  22.6 0.0 all-to-all-done.incoming
  22.6 3.3 %down.1 = f32[16,2048]{1,0:T(8,128)} custom-call(f32[16,24,128]{2,1,0:T(8,128)S(1)} %all-to-all-done.incoming, bf16[20,128,128]{2,1,0:T(8,128)(2,1)S(1)} %get-tuple-element.14.far_high, bf16[20,128,128]{2,1,0:T(8,128)(2,1)S(1)} %get-tuple-element.15.far_low, bf16[4,8,128,128]{3,2,1,0:T(8,128)(2,1)S(1)} %get-tuple-element.16.weights, ...), custom_call_target="tpu_custom_call" | custom-call | tf_op jit(solution)/shard_map/down/pallas_call | solution.py:586
Async XLA Ops:
  3.6 19.0 %all-to-all-start = ((f32[16,24,128]{2,1,0:T(8,128)}), f32[16,24,128]{2,1,0:T(8,128)S(1)}, u32[]{:S(2)}, u32[]{:S(2)}) async-start(f32[16,24,128]{2,1,0:T(8,128)} %get-tuple-element.12), calls=%async_computation | async-start | bytes 393216 | tf_op jit(solution)/shard_map/all_to_all | solution.py:534
  11.0 3.7 %collective-permute-start = (f32[16,1024]{1,0:T(8,128)S(1)}, f32[16,1024]{1,0:T(8,128)S(1)}, u32[]{:S(2)}, u32[]{:S(2)}) collective-permute-start(f32[16,1024]{1,0:T(8,128)S(1)} %get-tuple-element.13), channel_id=1, source_target_pairs={{0,1},{1,0},{2,3},{3,2},{4,5},{5,4},{6,7},{7,6},{8,9},{9,8},{10,11... | collective-permute-start | bytes 196616 | tf_op jit(solution)/shard_map/ppermute | solution.py:535
  11.1 8.3 %collective-permute-start.1 = (f32[16,1024]{1,0:T(8,128)S(1)}, f32[16,1024]{1,0:T(8,128)S(1)}, u32[]{:S(2)}, u32[]{:S(2)}) collective-permute-start(f32[16,1024]{1,0:T(8,128)S(1)} %get-tuple-element.17), channel_id=1, source_target_pairs={{1,2},{3,4},{5,6},{7,8},{9,10},{11,12},{13,14},{2,1},{4,3},{6,5},{... | collective-permute-start | bytes 196616 | tf_op jit(solution)/shard_map/ppermute | solution.py:537

commit v3 on v2

--- a/solution.py
+++ b/solution.py
@@ -12,6 +12,7 @@
 F32 = jnp.float32
 BF16 = jnp.bfloat16
 MIB = 1 << 20
+AHEAD = 4
 
 
 def split(x):
@@ -79,10 +80,16 @@
     trans_far,
     send_node_far,
     send_count_far,
+    upper_trans_far,
+    upper_coup_far,
     outgoing,
     sub_half,
     cross_half,
     weights,
+    upper_high,
+    upper_low,
+    upper_trans,
+    couplers,
     vec,
     basis,
     trans,
@@ -90,6 +97,7 @@
     send_count,
     rolled,
     semaphores,
+    upper_semaphores,
 ):
     position = lax.axis_index(BRANCH)
     half = vec.shape[1] // 2
@@ -101,6 +109,12 @@
         (vec, basis, trans, send_node, send_count, sub_half, cross_half),
         semaphores,
     )
+    sources = [upper_trans_far]
+    targets = [upper_trans]
+    for j in range(couplers.shape[0]):
+        sources.append(upper_coup_far.at[2 * members - 2 * (members >> j) + (position >> j)])
+        targets.append(couplers.at[j])
+    upper_arriving = fetch(sources, targets, upper_semaphores)
     basis_high, basis_low, trans_high, trans_low = (weights.at[i] for i in range(4))
     leaf_dev, rank, leaf_size = basis.shape
     vecs = vec.shape[0]
@@ -129,6 +143,9 @@
         level.append(joined(first, second, basis_high[g], basis_low[g]))
         keep(g, level[g])
     arriving[2].wait()
+    for copy in upper_arriving:
+        copy.wait()
+    tops = map_tops(members, upper_trans, couplers, upper_high, upper_low)
     for node in range(leaf_dev):
         group, q = node // 4, node % 4
         if node < leaf_dev - 1:
@@ -148,8 +165,12 @@
             weight += 1
             done += 1
         level = nodes
+        next(tops, None)
     two = jnp.where(left, times(level[0], trans_high[weight], trans_low[weight], contract_nt), 0.0)
+    next(tops, None)
     top = times(two, trans_high[weight], trans_low[weight], contract_nt)
+    for _ in tops:
+        pass
     keep(done, jnp.where(left, two, top))
     blank_index = 4 * (done + 1)
     rolled[blank_index] = jnp.zeros((vecs, LANES), F32)
@@ -182,62 +203,65 @@
     arriving[6].wait()
 
 
-def prepare(members, slots, coup_mat, upper_trans, upper_coup, far_high, far_low):
+def pack_couplings(members, slots, coup_mat, coup):
+    def one(source):
+        blocks = [coup_mat[source * slots + j] for j in range(slots)]
+        coup[0, source], coup[1, source] = split(jnp.concatenate(blocks, axis=1))
+
+    over(members, one)
+
+
+def map_tops(members, upper_trans, couplers, upper_high, upper_low):
     position = lax.axis_index(BRANCH)
-    rank = coup_mat.shape[1]
+    rank = upper_trans.shape[1]
     height = members.bit_length() - 1
-
-    def one(source):
-        for j in range(slots):
-            pieces = [coup_mat[source * slots + j]]
-            if j > 0:
-                pieces.insert(0, jnp.zeros((rank, j * rank), F32))
-            if j < slots - 1:
-                pieces.append(jnp.zeros((rank, (slots - 1 - j) * rank), F32))
-            high, low = split(jnp.concatenate(pieces, axis=1))
-            far_high[source, j * rank : (j + 1) * rank] = high
-            far_low[source, j * rank : (j + 1) * rank] = low
-
-    over(members, one)
-
-    nothing = jnp.zeros((members // 4, LANES, LANES), BF16)
-    far_high[members:] = nothing
-    far_low[members:] = nothing
+    upper_high[...] = jnp.zeros(upper_high.shape, BF16)
+    upper_low[...] = jnp.zeros(upper_low.shape, BF16)
     blank = jnp.zeros((rank, LANES - rank), F32)
 
     def place(group, value):
         high, low = split(value)
-        far_high[members + group, 2 * rank : 3 * rank] = high
-        far_low[members + group, 2 * rank : 3 * rank] = low
-
+        upper_high[group, 2 * rank : 3 * rank] = high
+        upper_low[group, 2 * rank : 3 * rank] = low
+
+    def transfer(index, c):
+        return upper_trans[index * 2 + c]
+
+    def child(j):
+        mixer = members - (members >> (j - 1)) + (position >> j)
+        return transfer(mixer, (position >> (j - 1)) & 1)
+
+    paths = [None, child(1)]
+    current = [[(position ^ 1, couplers[0])]] + [None] * (height - 1)
+    left_to_do = list(range(height))
+    while any(left_to_do[1:]) or any(entry is None for entry in current):
+        for j in range(1, height):
+            if current[j] is not None and left_to_do[j] > 0:
+                lower = left_to_do[j]
+                offset = members - (members >> (lower - 1))
+                following = []
+                for index, matrix in current[j]:
+                    for c in range(2):
+                        mixed = product(matrix, transfer(offset + index, c), contract_nn)
+                        following.append((2 * index + c, mixed))
+                current[j] = following
+                left_to_do[j] = lower - 1
+        for j in range(1, min(len(paths), height)):
+            if current[j] is None:
+                current[j] = [((position >> j) ^ 1, product(paths[j], couplers[j], contract_tn))]
+        if len(paths) < height:
+            paths.append(product(child(len(paths)), paths[-1], contract_nn))
+        yield
     own = jnp.zeros((rank, LANES), F32)
-    path = None
     for j in range(height):
-        number = members >> j
-        node = position >> j
-        if j > 0:
-            mixer = members - (members >> (j - 1)) + node
-            step = upper_trans[mixer * 2 + ((position >> (j - 1)) & 1)]
-            path = step if path is None else product(step, path, contract_nn)
-        coupler = upper_coup[2 * members - 2 * number + node]
-        start = coupler if path is None else product(path, coupler, contract_tn)
-        current = [(node ^ 1, start)]
-        for lower in range(j, 0, -1):
-            offset = members - (members >> (lower - 1))
-            following = []
-            for index, matrix in current:
-                for c in range(2):
-                    mixed = product(matrix, upper_trans[(offset + index) * 2 + c], contract_nn)
-                    following.append((2 * index + c, mixed))
-            current = following
         if j < 2:
-            for index, matrix in current:
+            for index, matrix in current[j]:
                 wide = jnp.concatenate([matrix, blank], axis=1)
                 own = own + pltpu.roll(wide, (index & 3) * rank, 1)
         else:
-            for k in range(0, len(current), 4):
-                wide = jnp.concatenate([matrix for _, matrix in current[k : k + 4]], axis=1)
-                place(current[k][0] >> 2, wide)
+            for k in range(0, len(current[j]), 4):
+                wide = jnp.concatenate([matrix for _, matrix in current[j][k : k + 4]], axis=1)
+                place(current[j][k][0] >> 2, wide)
     place(position >> 2, own)
 
 
@@ -256,15 +280,17 @@
     values,
     semaphores,
     block_semaphores,
+    ahead,
     before,
 ):
     position = lax.axis_index(BRANCH)
     leaves, near_slots, leaf_size, _ = near_mat.shape
-    leaf_dev = 2 * leaves
+    leaf_dev = near_src.shape[1]
     vecs = vec.shape[0]
     halo = leaf_dev // 2
     upper = (position & 1) ^ (1 if first else 0)
-    base = upper * leaves
+    base = upper * halo
+    skip = 0 if first else ahead.shape[0]
     arriving = fetch((vec_far, near_src_far, near_count_far), (vec, near_src, near_count), semaphores)
     chunks = block_semaphores.shape[0]
     chunk = leaves // chunks
@@ -272,11 +298,15 @@
     def chunk_copy(k):
         here = pl.ds(k * chunk, chunk)
         return pltpu.make_async_copy(
-            near_mat_far.at[pl.ds(base + k * chunk, chunk)], near_mat.at[here], block_semaphores.at[k]
+            near_mat_far.at[pl.ds(base + skip + k * chunk, chunk)], near_mat.at[here], block_semaphores.at[k]
         )
 
     for k in range(chunks):
         chunk_copy(k).start()
+    if first:
+        others = near_mat_far.at[pl.ds(halo - base, ahead.shape[0])]
+        ahead_copy = pltpu.make_async_copy(others, ahead, semaphores.at[len(arriving)])
+        ahead_copy.start()
     before()
     for copy in arriving:
         copy.wait()
@@ -301,7 +331,7 @@
         live = slot < near_count[0, base + leaf]
         return values[jnp.where(live, near_src[slot, base + leaf] + shift, 2 * leaf_dev)]
 
-    def two_leaves(pair):
+    def two_leaves(pair, blocks, start):
         total = None
         leaves = (2 * pair, 2 * pair + 1)
         for tile in range(0, near_slots, 4):
@@ -314,11 +344,12 @@
                 for i in range(tile, tile + columns, 2):
                     if i + 1 < tile + columns:
                         xs.append(jnp.where(wide_left, source(leaf, i), source(leaf, i + 1)))
-                        ws.append(jnp.concatenate([near_mat[leaf, i], near_mat[leaf, i + 1]], axis=1))
+                        two = [blocks[leaf - start, i], blocks[leaf - start, i + 1]]
+                        ws.append(jnp.concatenate(two, axis=1))
                     else:
                         xs.append(source(leaf, i))
                         blank = jnp.zeros((leaf_size, LANES - leaf_size), F32)
-                        ws.append(jnp.concatenate([near_mat[leaf, i], blank], axis=1))
+                        ws.append(jnp.concatenate([blocks[leaf - start, i], blank], axis=1))
                 rows_x.append(jnp.concatenate(xs, axis=1) if len(xs) > 1 else xs[0])
                 rows_w.append(jnp.concatenate(ws, axis=1) if len(ws) > 1 else ws[0])
             x = jnp.concatenate(rows_x, axis=0)
@@ -330,10 +361,14 @@
         lanes = pl.ds(pl.multiple_of((base // 2 + pair) * LANES, LANES), LANES)
         near[:, lanes] = jnp.where(left, first, second)
 
+    for pair in range(skip // 2):
+        two_leaves(pair, ahead, 0)
     for k in range(chunks):
         chunk_copy(k).wait()
         for m in range(chunk // 2):
-            two_leaves(k * (chunk // 2) + m)
+            two_leaves(skip // 2 + k * (chunk // 2) + m, near_mat, skip)
+    if first:
+        ahead_copy.wait()
 
 
 def first_kernel(
@@ -345,61 +380,63 @@
     near_count_far,
     near_mat_far,
     coup_mat_far,
-    upper_trans_far,
-    upper_coup_far,
+    coup_tgt_far,
     near,
-    far_high,
-    far_low,
+    coup,
+    targets,
+    ahead,
     coup_mat,
-    upper_trans,
-    upper_coup,
-    prepare_semaphores,
+    coup_semaphores,
     *scratch,
 ):
-    arriving = fetch(
-        (upper_trans_far, upper_coup_far, coup_mat_far), (upper_trans, upper_coup, coup_mat), prepare_semaphores
-    )
+    arriving = fetch((coup_mat_far, coup_tgt_far), (coup_mat, targets), coup_semaphores)
 
     def before():
         for copy in arriving:
             copy.wait()
-        prepare(members, slots, coup_mat, upper_trans, upper_coup, far_high, far_low)
-
-    near_half(True, halo_half, vec_far, near_src_far, near_count_far, near_mat_far, near, *scratch, before)
-
-
-def second_kernel(halo_half, vec_far, near_src_far, near_count_far, near_mat_far, near_first, near, *scratch):
+        pack_couplings(members, slots, coup_mat, coup)
+
+    near_half(True, halo_half, vec_far, near_src_far, near_count_far, near_mat_far, near, *scratch, ahead, before)
+
+
+def second_kernel(
+    halo_half, vec_far, near_src_far, near_count_far, near_mat_far, near_first, ahead, near, *scratch
+):
     del near_first
-    near_half(
-        False, halo_half, vec_far, near_src_far, near_count_far, near_mat_far, near, *scratch, lambda: None
-    )
+    inputs = (halo_half, vec_far, near_src_far, near_count_far, near_mat_far)
+    near_half(False, *inputs, near, *scratch, ahead, lambda: None)
 
 
 def down_kernel(
     members,
     slots,
     incoming,
-    far_high,
-    far_low,
+    coup,
+    upper_high,
+    upper_low,
     weights,
     near,
-    coup_tgt_far,
+    targets,
     out,
     coup_tgt,
-    far,
+    parts_far,
     pieces,
     semaphores,
 ):
-    arriving = fetch((coup_tgt_far,), (coup_tgt,), semaphores)
+    arriving = fetch((targets,), (coup_tgt,), semaphores)
     basis_high, basis_low, trans_high, trans_low = (weights.at[i] for i in range(4))
     vecs = out.shape[0]
     rank = LANES // slots
-    groups = far.shape[0]
-    far[...] = jnp.zeros(far.shape, F32)
+    groups = parts_far.shape[1]
+    parts_far[...] = jnp.zeros(parts_far.shape, F32)
     part = lane_part(vecs, rank)
 
+    pieces[...] = jnp.zeros(pieces.shape, F32)
+
     def couple(source):
-        pieces[source] = times(incoming[source, :vecs], far_high[source], far_low[source], contract_nt)
+        values = incoming[source, :vecs]
+        rows = jnp.concatenate([jnp.where(part == j, values, 0.0) for j in range(slots)], axis=0)
+        pieces[source, :, :rank] = times(rows, coup[0, source], coup[1, source], contract_nt)
 
     over(members, couple)
 
@@ -413,17 +450,17 @@
             first = jnp.where(few == q, rows, first)
             second = jnp.where(few == (q + 1) % 4, rows, second)
         tops = jnp.concatenate([first, pltpu.roll(second, LANES - rank, 1)], axis=0)
-        term = term + times(tops, far_high[members + g], far_low[members + g], contract_nt)
+        term = term + times(tops, upper_high[g], upper_low[g], contract_nt)
     arriving[0].wait()
 
     def scatter(source):
-        piece = pieces[source]
         for j in range(slots):
             node = coup_tgt[j, source]
-            alone = jnp.where(part == j, piece, 0.0)
-            far[node >> 2] += pltpu.roll(alone, ((node - j) & 3) * rank, 1)
+            alone = pieces[source, j * vecs : (j + 1) * vecs]
+            parts_far[j, node >> 2] += pltpu.roll(alone, (node & 3) * rank, 1)
 
     over(members, scatter)
+    far = [sum(parts_far[j, g] for j in range(1, slots)) + parts_far[0, g] for g in range(groups)]
 
     left = part < 2
     weight = trans_high.shape[0] - 1
@@ -503,17 +540,22 @@
     def held(*dims):
         return shape(dims, BF16)
 
-    outgoing, sub_half, cross_half, weights = pl.pallas_call(
+    height = members.bit_length() - 1
+    outgoing, sub_half, cross_half, weights, upper_high, upper_low = pl.pallas_call(
         functools.partial(up_kernel, members, slots),
         out_shape=[
             shape((members, vecs + vecs // 2, LANES), F32),
             shape((vecs, points // 2), F32),
             shape((vecs, points // 2), F32),
             held(4, groups, LANES, LANES),
+            held(members // 4, LANES, LANES),
+            held(members // 4, LANES, LANES),
         ],
-        in_specs=[HBM_SPEC] * 5,
-        out_specs=[VMEM_SPEC] * 4,
+        in_specs=[HBM_SPEC] * 7,
+        out_specs=[VMEM_SPEC] * 6,
         scratch_shapes=[
+            pltpu.VMEM(upper_blocks.shape, F32),
+            pltpu.VMEM((height, rank, rank), F32),
             pltpu.VMEM((vecs, points), F32),
             pltpu.VMEM(basis.shape, F32),
             pltpu.VMEM(trans_blocks.shape, F32),
@@ -521,6 +563,7 @@
             pltpu.SMEM((1, members), jnp.int32),
             pltpu.VMEM((4 * node_groups + 8, vecs, LANES), F32),
             pltpu.SemaphoreType.DMA((7,)),
+            pltpu.SemaphoreType.DMA((1 + height,)),
         ],
         compiler_params=params(8 + members // 4),
         name="up",
@@ -530,79 +573,90 @@
         in_hbm(trans_blocks),
         in_hbm(jnp.transpose(send_node[0])),
         in_hbm(send_count),
+        in_hbm(upper_blocks),
+        in_hbm(upper_coup),
     )
     incoming = lax.all_to_all(outgoing, BRANCH, split_axis=0, concat_axis=0, tiled=True)
     sub_got = lax.ppermute(sub_half, BRANCH, [(i, i ^ 1) for i in range(members)])
     pairs = [(i, i + 1) for i in range(1, members - 1, 2)]
     cross_got = lax.ppermute(cross_half, BRANCH, pairs + [(b, a) for a, b in pairs])
 
-    near_scratch = [
-        pltpu.VMEM((vecs, points), F32),
-        pltpu.SMEM(near_src.shape[::-1], jnp.int32),
-        pltpu.SMEM((1, leaf_dev), jnp.int32),
-        pltpu.VMEM((leaf_dev // 2,) + near_mat.shape[1:], F32),
-        pltpu.VMEM((2 * leaf_dev + 1, 2 * vecs, LANES), BF16),
-        pltpu.SemaphoreType.DMA((3,)),
-        pltpu.SemaphoreType.DMA((near_chunks,)),
-    ]
+    def near_scratch(leaves):
+        return [
+            pltpu.VMEM((vecs, points), F32),
+            pltpu.SMEM(near_src.shape[::-1], jnp.int32),
+            pltpu.SMEM((1, leaf_dev), jnp.int32),
+            pltpu.VMEM((leaves,) + near_mat.shape[1:], F32),
+            pltpu.VMEM((2 * leaf_dev + 1, 2 * vecs, LANES), BF16),
+            pltpu.SemaphoreType.DMA((4,)),
+            pltpu.SemaphoreType.DMA((near_chunks,)),
+        ]
+
+    ahead_leaves = AHEAD
     near_inputs = (
         in_hbm(vectors),
         in_hbm(jnp.transpose(near_src)),
         in_hbm(near_count.reshape(1, -1)),
         in_hbm(near_mat),
     )
-    near, far_high, far_low = pl.pallas_call(
+    near, coup, targets, ahead = pl.pallas_call(
         functools.partial(first_kernel, members, slots),
         out_shape=[
             shape((vecs, points), F32),
-            held(members + members // 4, LANES, LANES),
-            held(members + members // 4, LANES, LANES),
+            held(2, members, rank, LANES),
+            shape((slots, members), jnp.int32),
+            shape((ahead_leaves,) + near_mat.shape[1:], F32),
         ],
-        in_specs=[VMEM_SPEC] + [HBM_SPEC] * 7,
-        out_specs=[VMEM_SPEC] * 3,
+        in_specs=[VMEM_SPEC] + [HBM_SPEC] * 6,
+        out_specs=[VMEM_SPEC] * 4,
         scratch_shapes=[
             pltpu.VMEM(coup_blocks.shape, F32),
-            pltpu.VMEM(upper_blocks.shape, F32),
-            pltpu.VMEM(upper_coup.shape, F32),
-            pltpu.SemaphoreType.DMA((3,)),
+            pltpu.SemaphoreType.DMA((2,)),
         ]
-        + near_scratch,
+        + near_scratch(leaf_dev // 2),
         compiler_params=params(12 + members // 4),
         cost_estimate=cost(1 << 28, 16 << 20),
         name="near_first",
-    )(sub_got, *near_inputs, in_hbm(coup_blocks), in_hbm(upper_blocks), in_hbm(upper_coup))
+    )(
+        sub_got,
+        *near_inputs,
+        in_hbm(coup_blocks),
+        in_hbm(jnp.transpose(coup_tgt[0])),
+    )
+
     near = pl.pallas_call(
         second_kernel,
         out_shape=shape((vecs, points), F32),
-        in_specs=[VMEM_SPEC] + [HBM_SPEC] * 4 + [VMEM_SPEC],
+        in_specs=[VMEM_SPEC] + [HBM_SPEC] * 4 + [VMEM_SPEC] * 2,
         out_specs=VMEM_SPEC,
-        scratch_shapes=near_scratch,
+        scratch_shapes=near_scratch(leaf_dev // 2 - ahead_leaves),
         input_output_aliases={5: 0},
-        compiler_params=params(12),
+        compiler_params=params(12 + members // 4),
         cost_estimate=cost(1 << 28, 8 << 20),
         name="near_second",
-    )(cross_got, *near_inputs, near)
+    )(cross_got, *near_inputs, near, ahead)
 
     return pl.pallas_call(
         functools.partial(down_kernel, members, slots),
         out_shape=shape((vecs, points), F32),
-        in_specs=[VMEM_SPEC] * 5 + [HBM_SPEC],
+        in_specs=[VMEM_SPEC] * 7,
         out_specs=VMEM_SPEC,
         scratch_shapes=[
             pltpu.SMEM((slots, members), jnp.int32),
-            pltpu.VMEM((node_groups, vecs, LANES), F32),
-            pltpu.VMEM((members, vecs, LANES), F32),
+            pltpu.VMEM((slots, node_groups, vecs, LANES), F32),
+            pltpu.VMEM((members, slots * vecs, LANES), F32),
             pltpu.SemaphoreType.DMA((1,)),
         ],
         compiler_params=params(8 + members // 4),
         name="down",
     )(
         incoming,
-        far_high,
-        far_low,
+        coup,
+        upper_high,
+        upper_low,
         weights,
         near,
-        in_hbm(jnp.transpose(coup_tgt[0])),
+        targets,
     )
 
 

time: 26.2 us -> 24.3 us (0.927)
  Pallas kernels: 14.8 us -> 13 us
    pallas_call x1, Pallas kernels: 4.77 us -> 3.52 us  [body(): pl.pallas_call(functools.partial(first_kernel, members, slots), out_shape...]
    pallas_call x1, Pallas kernels: 3.28 us -> 2.6 us  [body(): pl.pallas_call(functools.partial(down_kernel, members, slots), out_shape=...]
    pallas_call x1, Pallas kernels: 3.64 us -> 4.01 us  [body(): pl.pallas_call(functools.partial(up_kernel, members, slots), out_shape=[s...]
    pallas_call x1, Pallas kernels: 3.16 us -> 2.84 us  [body(): pl.pallas_call(second_kernel, out_shape=shape((vecs, points), F32), in_sp...]
  transfers between devices with their start and end apart: 3 -> 3, of which waited for: 0 -> 0; matrix products, arithmetic and copies ran while one was open for 0% -> 0% of each run, Pallas kernels for 31% -> 27%
where the time goes in v3:
time: 24.3 us; the launch traced here: 24 us
  Pallas kernels  13 us (53%)
  starting transfers between devices  11 us (45%)
    all_to_all x1, starting transfers between devices, body(): lax.all_to_all(outgoing, BRANCH, split_axis=0, concat_axis=0, tiled=True)  7.33 us
    pallas_call x1, Pallas kernels, body(): pl.pallas_call(functools.partial(up_kernel, members, slots), out_shape=[s...  4.01 us
    pallas_call x1, Pallas kernels, body(): pl.pallas_call(functools.partial(first_kernel, members, slots), out_shape...  3.52 us
    ppermute x1, starting transfers between devices, body(): lax.ppermute(cross_half, BRANCH, pairs + [(b, a) for a, b in pairs])  3.51 us
    pallas_call x1, Pallas kernels, body(): pl.pallas_call(second_kernel, out_shape=shape((vecs, points), F32), in_sp...  2.84 us
    pallas_call x1, Pallas kernels, body(): pl.pallas_call(functools.partial(down_kernel, members, slots), out_shape=...  2.6 us
  transfers between devices with their start and end apart: 3, of which 0 were waited for; matrix products, arithmetic and copies ran while one was open for 0% of the time, Pallas kernels for 27%

profile of v3, /device:TPU:1, one launch (start us, length us, event | category | flops | bytes accessed | tf_op | source)
XLA Modules:
  0.0 24.0 jit_solution(15562373730416480548)
XLA Ops:
  0.0 4.0 %up.1 = (f32[16,24,128]{2,1,0:T(8,128)}, f32[16,1024]{1,0:T(8,128)S(1)}, f32[16,1024]{1,0:T(8,128)S(1)}, bf16[4,8,128,128]{3,2,1,0:T(8,128)(2,1)S(1)}, bf16[4,12...) custom-call(f32[16,2048]{1,0:T(8,128)} %vec_far.5, f32[32,32,64]{2,1,0:T(8,128)} %basis_far.1, ...), custom_call_target="tpu_custom_call" | custom-call | tf_op jit(solution)/shard_map/up/pallas_call | solution.py:544
  4.0 7.3 %all-to-all-start = ((f32[16,24,128]{2,1,0:T(8,128)}), f32[16,24,128]{2,1,0:T(8,128)S(1)}, u32[]{:S(2)}, u32[]{:S(2)}) async-start(f32[16,24,128]{2,1,0:T(8,128)} %get-tuple-element.15), calls=%async_computation | async-start | bytes 393216 | tf_op jit(solution)/shard_map/all_to_all | solution.py:579
  11.4 0.2 collective-permute-start
  11.5 3.5 %collective-permute-start.1 = (f32[16,1024]{1,0:T(8,128)S(1)}, f32[16,1024]{1,0:T(8,128)S(1)}, u32[]{:S(2)}, u32[]{:S(2)}) collective-permute-start(f32[16,1024]{1,0:T(8,128)S(1)} %get-tuple-element.21), channel_id=1, source_target_pairs={{1,2},{3,4},{5,6},{7,8},{9,10},{11,12},{13,14},{2,1},{4,3},{6,5},{... | collective-permute-start | bytes 196616 | tf_op jit(solution)/shard_map/ppermute | solution.py:582
  15.0 0.0 collective-permute-done.halo_half
  15.1 3.5 %near_first.1 = (f32[16,2048]{1,0:T(8,128)S(1)}, bf16[2,16,32,128]{3,2,1,0:T(8,128)(2,1)S(1)}, s32[4,16]{1,0:T(4,128)S(1)}, f32[4,9,64,64]{3,2,1,0:T(8,128)S(1)}) custom-call(f32[16,1024]{1,0:T(8,128)S(1)} %collective-permute-done.halo_half, f32[16,2048]{1,0:T(8,128)} %vec_far.5, s32[9,32]{1,0:T(8,128)} %bitcast.14, s32[1,32]{1,0:T(1,128)} %bitcast.18, ...), custom_call_target="tpu_custom_call" | custom-call | flops 268435456 | bytes 16777216 | tf_op jit(solution)/shard_map/near_first/pallas_call | solution.py:602
  18.6 0.0 collective-permute-done.1.halo_half
  18.6 2.8 %near_second.1.near = f32[16,2048]{1,0:T(8,128)S(1)} custom-call(f32[16,1024]{1,0:T(8,128)S(1)} %collective-permute-done.1.halo_half, f32[16,2048]{1,0:T(8,128)} %vec_far.5, s32[9,32]{1,0:T(8,128)} %bitcast.15, s32[1,32]{1,0:T(1,128)} %bitcast.19, f32[32,9,64,64]{3,2,1,0:T(8,128)} %near_mat_far.3, ...), custom_call_target="tpu_custom_call", output_to_operand_aliasing={{}: (5, {})} | custom-call | flops 268435456 | bytes 8388608 | tf_op jit(solution)/shard_map/near_second/pallas_call | solution.py:627
  21.4 0.0 all-to-all-done.incoming
  21.4 2.6 %down.1 = f32[16,2048]{1,0:T(8,128)} custom-call(f32[16,24,128]{2,1,0:T(8,128)S(1)} %all-to-all-done.incoming, bf16[2,16,32,128]{3,2,1,0:T(8,128)(2,1)S(1)} %get-tuple-element.17.coup, bf16[4,128,128]{2,1,0:T(8,128)(2,1)S(1)} %get-tuple-element.18.upper_high, bf16[4,128,128]{2,1,0:T(8,128)(2,1)S(1)} %get-tuple-element.19.upper_low, ...), custom_call_target="tpu_custom_call" | custom-call | tf_op jit(solution)/shard_map/down/pallas_call | solution.py:639
Async XLA Ops:
  4.0 17.4 %all-to-all-start = ((f32[16,24,128]{2,1,0:T(8,128)}), f32[16,24,128]{2,1,0:T(8,128)S(1)}, u32[]{:S(2)}, u32[]{:S(2)}) async-start(f32[16,24,128]{2,1,0:T(8,128)} %get-tuple-element.15), calls=%async_computation | async-start | bytes 393216 | tf_op jit(solution)/shard_map/all_to_all | solution.py:579
  11.4 3.7 %collective-permute-start = (f32[16,1024]{1,0:T(8,128)S(1)}, f32[16,1024]{1,0:T(8,128)S(1)}, u32[]{:S(2)}, u32[]{:S(2)}) collective-permute-start(f32[16,1024]{1,0:T(8,128)S(1)} %get-tuple-element.16), channel_id=1, source_target_pairs={{0,1},{1,0},{2,3},{3,2},{4,5},{5,4},{6,7},{7,6},{8,9},{9,8},{10,11... | collective-permute-start | bytes 196616 | tf_op jit(solution)/shard_map/ppermute | solution.py:580
  11.5 7.1 %collective-permute-start.1 = (f32[16,1024]{1,0:T(8,128)S(1)}, f32[16,1024]{1,0:T(8,128)S(1)}, u32[]{:S(2)}, u32[]{:S(2)}) collective-permute-start(f32[16,1024]{1,0:T(8,128)S(1)} %get-tuple-element.21), channel_id=1, source_target_pairs={{1,2},{3,4},{5,6},{7,8},{9,10},{11,12},{13,14},{2,1},{4,3},{6,5},{... | collective-permute-start | bytes 196616 | tf_op jit(solution)/shard_map/ppermute | solution.py:582

commit v4 on v3

--- a/solution.py
+++ b/solution.py
@@ -12,7 +12,7 @@
 F32 = jnp.float32
 BF16 = jnp.bfloat16
 MIB = 1 << 20
-AHEAD = 4
+AHEAD = 6
 
 
 def split(x):
@@ -86,8 +86,7 @@
     sub_half,
     cross_half,
     weights,
-    upper_high,
-    upper_low,
+    upper,
     upper_trans,
     couplers,
     vec,
@@ -145,7 +144,9 @@
     arriving[2].wait()
     for copy in upper_arriving:
         copy.wait()
-    tops = map_tops(members, upper_trans, couplers, upper_high, upper_low)
+    arriving[3].wait()
+    arriving[4].wait()
+    tops = map_tops(members, upper_trans, couplers, upper)
     for node in range(leaf_dev):
         group, q = node // 4, node % 4
         if node < leaf_dev - 1:
@@ -175,8 +176,6 @@
     blank_index = 4 * (done + 1)
     rolled[blank_index] = jnp.zeros((vecs, LANES), F32)
 
-    arriving[3].wait()
-    arriving[4].wait()
     part = lane_part(vecs, rank)
     few = lane_part(vecs // 2, rank)
     first = position & 3
@@ -211,18 +210,14 @@
     over(members, one)
 
 
-def map_tops(members, upper_trans, couplers, upper_high, upper_low):
+def map_tops(members, upper_trans, couplers, upper):
     position = lax.axis_index(BRANCH)
     rank = upper_trans.shape[1]
     height = members.bit_length() - 1
-    upper_high[...] = jnp.zeros(upper_high.shape, BF16)
-    upper_low[...] = jnp.zeros(upper_low.shape, BF16)
     blank = jnp.zeros((rank, LANES - rank), F32)
 
     def place(group, value):
-        high, low = split(value)
-        upper_high[group, 2 * rank : 3 * rank] = high
-        upper_low[group, 2 * rank : 3 * rank] = low
+        upper[0, group], upper[1, group] = split(value)
 
     def transfer(index, c):
         return upper_trans[index * 2 + c]
@@ -292,16 +287,14 @@
     base = upper * halo
     skip = 0 if first else ahead.shape[0]
     arriving = fetch((vec_far, near_src_far, near_count_far), (vec, near_src, near_count), semaphores)
-    chunks = block_semaphores.shape[0]
-    chunk = leaves // chunks
+    sizes = ((leaves + 3) // 4 * 2, leaves - (leaves + 3) // 4 * 2)
 
     def chunk_copy(k):
-        here = pl.ds(k * chunk, chunk)
-        return pltpu.make_async_copy(
-            near_mat_far.at[pl.ds(base + skip + k * chunk, chunk)], near_mat.at[here], block_semaphores.at[k]
-        )
-
-    for k in range(chunks):
+        start = k * sizes[0]
+        there = near_mat_far.at[pl.ds(base + skip + start, sizes[k])]
+        return pltpu.make_async_copy(there, near_mat.at[pl.ds(start, sizes[k])], block_semaphores.at[k])
+
+    for k in range(2):
         chunk_copy(k).start()
     if first:
         others = near_mat_far.at[pl.ds(halo - base, ahead.shape[0])]
@@ -363,10 +356,10 @@
 
     for pair in range(skip // 2):
         two_leaves(pair, ahead, 0)
-    for k in range(chunks):
+    for k in range(2):
         chunk_copy(k).wait()
-        for m in range(chunk // 2):
-            two_leaves(skip // 2 + k * (chunk // 2) + m, near_mat, skip)
+        for m in range(sizes[k] // 2):
+            two_leaves((skip + k * sizes[0]) // 2 + m, near_mat, skip)
     if first:
         ahead_copy.wait()
 
@@ -412,8 +405,7 @@
     slots,
     incoming,
     coup,
-    upper_high,
-    upper_low,
+    upper,
     weights,
     near,
     targets,
@@ -441,7 +433,7 @@
     over(members, couple)
 
     few = lane_part(vecs // 2, rank)
-    term = jnp.zeros((vecs, LANES), F32)
+    term = jnp.zeros((vecs, rank), F32)
     for g in range(members // 4):
         first = jnp.zeros((vecs // 2, LANES), F32)
         second = jnp.zeros((vecs // 2, LANES), F32)
@@ -450,7 +442,9 @@
             first = jnp.where(few == q, rows, first)
             second = jnp.where(few == (q + 1) % 4, rows, second)
         tops = jnp.concatenate([first, pltpu.roll(second, LANES - rank, 1)], axis=0)
-        term = term + times(tops, upper_high[g], upper_low[g], contract_nt)
+        term = term + times(tops, upper[0, g], upper[1, g], contract_nt)
+    sides = [jnp.zeros((vecs, 2 * rank), F32), term, jnp.zeros((vecs, rank), F32)]
+    term = jnp.concatenate(sides, axis=1)
     arriving[0].wait()
 
     def scatter(source):
@@ -534,25 +528,23 @@
     trans_blocks = trans.reshape(-1, rank, rank)
     coup_blocks = coup_mat.reshape(-1, rank, rank)
     upper_blocks = upper_trans.reshape(-1, rank, rank)
-    near_chunks = leaf_dev // 16
     shape = jax.ShapeDtypeStruct
 
     def held(*dims):
         return shape(dims, BF16)
 
     height = members.bit_length() - 1
-    outgoing, sub_half, cross_half, weights, upper_high, upper_low = pl.pallas_call(
+    outgoing, sub_half, cross_half, weights, upper = pl.pallas_call(
         functools.partial(up_kernel, members, slots),
         out_shape=[
             shape((members, vecs + vecs // 2, LANES), F32),
             shape((vecs, points // 2), F32),
             shape((vecs, points // 2), F32),
             held(4, groups, LANES, LANES),
-            held(members // 4, LANES, LANES),
-            held(members // 4, LANES, LANES),
+            held(2, members // 4, rank, LANES),
         ],
         in_specs=[HBM_SPEC] * 7,
-        out_specs=[VMEM_SPEC] * 6,
+        out_specs=[VMEM_SPEC] * 5,
         scratch_shapes=[
             pltpu.VMEM(upper_blocks.shape, F32),
             pltpu.VMEM((height, rank, rank), F32),
@@ -589,7 +581,7 @@
             pltpu.VMEM((leaves,) + near_mat.shape[1:], F32),
             pltpu.VMEM((2 * leaf_dev + 1, 2 * vecs, LANES), BF16),
             pltpu.SemaphoreType.DMA((4,)),
-            pltpu.SemaphoreType.DMA((near_chunks,)),
+            pltpu.SemaphoreType.DMA((2,)),
         ]
 
     ahead_leaves = AHEAD
@@ -639,7 +631,7 @@
     return pl.pallas_call(
         functools.partial(down_kernel, members, slots),
         out_shape=shape((vecs, points), F32),
-        in_specs=[VMEM_SPEC] * 7,
+        in_specs=[VMEM_SPEC] * 6,
         out_specs=VMEM_SPEC,
         scratch_shapes=[
             pltpu.SMEM((slots, members), jnp.int32),
@@ -652,8 +644,7 @@
     )(
         incoming,
         coup,
-        upper_high,
-        upper_low,
+        upper,
         weights,
         near,
         targets,

time: 24.3 us -> 24 us (0.988)
  Pallas kernels: 13 us -> 12.7 us
  transfers between devices with their start and end apart: 3 -> 3, of which waited for: 0 -> 0; matrix products, arithmetic and copies ran while one was open for 0% -> 0% of each run, Pallas kernels for 27% -> 26%
where the time goes in v4:
time: 24 us; the launch traced here: 23.7 us
  Pallas kernels  12.7 us (53%)
  starting transfers between devices  11 us (46%)
    all_to_all x1, starting transfers between devices, body(): lax.all_to_all(outgoing, BRANCH, split_axis=0, concat_axis=0, tiled=True)  7.33 us
    pallas_call x1, Pallas kernels, body(): pl.pallas_call(functools.partial(up_kernel, members, slots), out_shape=[s...  3.89 us
    pallas_call x1, Pallas kernels, body(): pl.pallas_call(functools.partial(first_kernel, members, slots), out_shape...  3.52 us
    ppermute x1, starting transfers between devices, body(): lax.ppermute(cross_half, BRANCH, pairs + [(b, a) for a, b in pairs])  3.51 us
    pallas_call x1, Pallas kernels, body(): pl.pallas_call(second_kernel, out_shape=shape((vecs, points), F32), in_sp...  2.7 us
    pallas_call x1, Pallas kernels, body(): pl.pallas_call(functools.partial(down_kernel, members, slots), out_shape=...  2.54 us
  transfers between devices with their start and end apart: 3, of which 0 were waited for; matrix products, arithmetic and copies ran while one was open for 0% of the time, Pallas kernels for 26%

profile of v4, /device:TPU:1, one launch (start us, length us, event | category | flops | bytes accessed | tf_op | source)
XLA Modules:
  0.0 23.7 jit_solution(4137926538083007725)
XLA Ops:
  0.0 3.9 %up.1 = (f32[16,24,128]{2,1,0:T(8,128)}, f32[16,1024]{1,0:T(8,128)S(1)}, f32[16,1024]{1,0:T(8,128)S(1)}, bf16[4,8,128,128]{3,2,1,0:T(8,128)(2,1)S(1)}, bf16[2,4,32,128]{3,2,1,0:T(8,128)(2,1)S(1)}) custom-call(f32[16,2048]{1,0:T(8,128)} %vec_far.5, f32[32,32,64]{2,1,0:T(8,128)} %basis_far.1, f32[62,32,32]{2,1,0:T(8,128)} %bitcast.12, s32[4,16]{1,0:T(4,128)} %bitcast.16, ...), custom_call_target="tpu_custom_call" | custom-call | tf_op jit(solution)/shard_map/up/pallas_call | solution.py:537
  3.9 7.3 %all-to-all-start = ((f32[16,24,128]{2,1,0:T(8,128)}), f32[16,24,128]{2,1,0:T(8,128)S(1)}, u32[]{:S(2)}, u32[]{:S(2)}) async-start(f32[16,24,128]{2,1,0:T(8,128)} %get-tuple-element.14), calls=%async_computation | async-start | bytes 393216 | tf_op jit(solution)/shard_map/all_to_all | solution.py:571
  11.2 0.2 collective-permute-start
  11.4 3.5 %collective-permute-start.1 = (f32[16,1024]{1,0:T(8,128)S(1)}, f32[16,1024]{1,0:T(8,128)S(1)}, u32[]{:S(2)}, u32[]{:S(2)}) collective-permute-start(f32[16,1024]{1,0:T(8,128)S(1)} %get-tuple-element.19), channel_id=1, source_target_pairs={{1,2},{3,4},{5,6},{7,8},{9,10},{11,12},{13,14},{2,1},{4,3},{6,5},{... | collective-permute-start | bytes 196616 | tf_op jit(solution)/shard_map/ppermute | solution.py:574
  14.9 0.0 collective-permute-done.halo_half
  14.9 3.5 %near_first.1 = (f32[16,2048]{1,0:T(8,128)S(1)}, bf16[2,16,32,128]{3,2,1,0:T(8,128)(2,1)S(1)}, s32[4,16]{1,0:T(4,128)S(1)}, f32[6,9,64,64]{3,2,1,0:T(8,128)S(1)}) custom-call(f32[16,1024]{1,0:T(8,128)S(1)} %collective-permute-done.halo_half, f32[16,2048]{1,0:T(8,128)} %vec_far.5, s32[9,32]{1,0:T(8,128)} %bitcast.14, s32[1,32]{1,0:T(1,128)} %bitcast.18, ...), custom_call_target="tpu_custom_call" | custom-call | flops 268435456 | bytes 16777216 | tf_op jit(solution)/shard_map/near_first/pallas_call | solution.py:594
  18.5 0.0 collective-permute-done.1.halo_half
  18.5 2.7 %near_second.1.near = f32[16,2048]{1,0:T(8,128)S(1)} custom-call(f32[16,1024]{1,0:T(8,128)S(1)} %collective-permute-done.1.halo_half, f32[16,2048]{1,0:T(8,128)} %vec_far.5, s32[9,32]{1,0:T(8,128)} %bitcast.15, s32[1,32]{1,0:T(1,128)} %bitcast.19, f32[32,9,64,64]{3,2,1,0:T(8,128)} %near_mat_far.3, ...), custom_call_target="tpu_custom_call", output_to_operand_aliasing={{}: (5, {})} | custom-call | flops 268435456 | bytes 8388608 | tf_op jit(solution)/shard_map/near_second/pallas_call | solution.py:619
  21.2 0.0 all-to-all-done.incoming
  21.2 2.5 %down.1 = f32[16,2048]{1,0:T(8,128)} custom-call(f32[16,24,128]{2,1,0:T(8,128)S(1)} %all-to-all-done.incoming, bf16[2,16,32,128]{3,2,1,0:T(8,128)(2,1)S(1)} %get-tuple-element.16.coup, bf16[2,4,32,128]{3,2,1,0:T(8,128)(2,1)S(1)} %get-tuple-element.17.upper, bf16[4,8,128,128]{3,2,1,0:T(8,128)(2,1)S(1)} %get-tuple-element.18.weights, ...), custom_call_target="tpu_custom_call" | custom-call | tf_op jit(solution)/shard_map/down/pallas_call | solution.py:631
Async XLA Ops:
  3.9 17.3 %all-to-all-start = ((f32[16,24,128]{2,1,0:T(8,128)}), f32[16,24,128]{2,1,0:T(8,128)S(1)}, u32[]{:S(2)}, u32[]{:S(2)}) async-start(f32[16,24,128]{2,1,0:T(8,128)} %get-tuple-element.14), calls=%async_computation | async-start | bytes 393216 | tf_op jit(solution)/shard_map/all_to_all | solution.py:571
  11.2 3.7 %collective-permute-start = (f32[16,1024]{1,0:T(8,128)S(1)}, f32[16,1024]{1,0:T(8,128)S(1)}, u32[]{:S(2)}, u32[]{:S(2)}) collective-permute-start(f32[16,1024]{1,0:T(8,128)S(1)} %get-tuple-element.15), channel_id=1, source_target_pairs={{0,1},{1,0},{2,3},{3,2},{4,5},{5,4},{6,7},{7,6},{8,9},{9,8},{10,11... | collective-permute-start | bytes 196616 | tf_op jit(solution)/shard_map/ppermute | solution.py:572
  11.4 7.1 %collective-permute-start.1 = (f32[16,1024]{1,0:T(8,128)S(1)}, f32[16,1024]{1,0:T(8,128)S(1)}, u32[]{:S(2)}, u32[]{:S(2)}) collective-permute-start(f32[16,1024]{1,0:T(8,128)S(1)} %get-tuple-element.19), channel_id=1, source_target_pairs={{1,2},{3,4},{5,6},{7,8},{9,10},{11,12},{13,14},{2,1},{4,3},{6,5},{... | collective-permute-start | bytes 196616 | tf_op jit(solution)/shard_map/ppermute | solution.py:574

commit v5 on v4

--- a/solution.py
+++ b/solution.py
@@ -103,17 +103,19 @@
     start = (position & 1) * half
     at_partner = vec_far.at[:, pl.ds(pl.multiple_of(half - start, LANES), half)]
     at_neighbour = vec_far.at[:, pl.ds(pl.multiple_of(start, LANES), half)]
-    arriving = fetch(
-        (vec_far, basis_far, trans_far, send_node_far, send_count_far, at_partner, at_neighbour),
-        (vec, basis, trans, send_node, send_count, sub_half, cross_half),
-        semaphores,
-    )
+    wanted = fetch((vec_far, basis_far), (vec, basis), semaphores)
     sources = [upper_trans_far]
     targets = [upper_trans]
     for j in range(couplers.shape[0]):
         sources.append(upper_coup_far.at[2 * members - 2 * (members >> j) + (position >> j)])
         targets.append(couplers.at[j])
     upper_arriving = fetch(sources, targets, upper_semaphores)
+    others = fetch(
+        (trans_far, send_node_far, send_count_far, at_partner, at_neighbour),
+        (trans, send_node, send_count, sub_half, cross_half),
+        semaphores.at[pl.ds(2, 5)],
+    )
+    arriving = wanted + others
     basis_high, basis_low, trans_high, trans_low = (weights.at[i] for i in range(4))
     leaf_dev, rank, leaf_size = basis.shape
     vecs = vec.shape[0]
@@ -160,13 +162,13 @@
     weight = 0
     while len(level) > 1:
         nodes = []
+        next(tops, None)
         for g in range(len(level) // 2):
             nodes.append(joined(level[2 * g], level[2 * g + 1], trans_high[weight], trans_low[weight]))
             keep(done, nodes[g])
             weight += 1
             done += 1
         level = nodes
-        next(tops, None)
     two = jnp.where(left, times(level[0], trans_high[weight], trans_low[weight], contract_nt), 0.0)
     next(tops, None)
     top = times(two, trans_high[weight], trans_low[weight], contract_nt)
@@ -423,12 +425,13 @@
     parts_far[...] = jnp.zeros(parts_far.shape, F32)
     part = lane_part(vecs, rank)
 
-    pieces[...] = jnp.zeros(pieces.shape, F32)
+    blank = jnp.zeros((slots * vecs, LANES - rank), F32)
 
     def couple(source):
         values = incoming[source, :vecs]
         rows = jnp.concatenate([jnp.where(part == j, values, 0.0) for j in range(slots)], axis=0)
-        pieces[source, :, :rank] = times(rows, coup[0, source], coup[1, source], contract_nt)
+        narrow = times(rows, coup[0, source], coup[1, source], contract_nt)
+        pieces[source] = jnp.concatenate([narrow, blank], axis=1)
 
     over(members, couple)
 

time: 24 us -> 24 us (level)
  no operation moved by 1% of the time
where the time goes in v5:
time: 24 us; the launch traced here: 23.7 us
  Pallas kernels  12.7 us (53%)
  starting transfers between devices  11 us (46%)
    all_to_all x1, starting transfers between devices, body(): lax.all_to_all(outgoing, BRANCH, split_axis=0, concat_axis=0, tiled=True)  7.32 us
    pallas_call x1, Pallas kernels, body(): pl.pallas_call(functools.partial(up_kernel, members, slots), out_shape=[s...  3.88 us
    pallas_call x1, Pallas kernels, body(): pl.pallas_call(functools.partial(first_kernel, members, slots), out_shape...  3.53 us
    ppermute x1, starting transfers between devices, body(): lax.ppermute(cross_half, BRANCH, pairs + [(b, a) for a, b in pairs])  3.51 us
    pallas_call x1, Pallas kernels, body(): pl.pallas_call(second_kernel, out_shape=shape((vecs, points), F32), in_sp...  2.72 us
    pallas_call x1, Pallas kernels, body(): pl.pallas_call(functools.partial(down_kernel, members, slots), out_shape=...  2.53 us
  transfers between devices with their start and end apart: 3, of which 0 were waited for; matrix products, arithmetic and copies ran while one was open for 0% of the time, Pallas kernels for 26%

profile of v5, /device:TPU:1, one launch (start us, length us, event | category | flops | bytes accessed | tf_op | source)
XLA Modules:
  0.0 23.7 jit_solution(9471520505908679144)
XLA Ops:
  0.0 3.9 %up.1 = (f32[16,24,128]{2,1,0:T(8,128)}, f32[16,1024]{1,0:T(8,128)S(1)}, f32[16,1024]{1,0:T(8,128)S(1)}, bf16[4,8,128,128]{3,2,1,0:T(8,128)(2,1)S(1)}, bf16[2,4,32,128]{3,2,1,0:T(8,128)(2,1)S(1)}) custom-call(f32[16,2048]{1,0:T(8,128)} %vec_far.5, f32[32,32,64]{2,1,0:T(8,128)} %basis_far.1, f32[62,32,32]{2,1,0:T(8,128)} %bitcast.12, s32[4,16]{1,0:T(4,128)} %bitcast.16, ...), custom_call_target="tpu_custom_call" | custom-call | tf_op jit(solution)/shard_map/up/pallas_call | solution.py:540
  3.9 7.3 %all-to-all-start = ((f32[16,24,128]{2,1,0:T(8,128)}), f32[16,24,128]{2,1,0:T(8,128)S(1)}, u32[]{:S(2)}, u32[]{:S(2)}) async-start(f32[16,24,128]{2,1,0:T(8,128)} %get-tuple-element.14), calls=%async_computation | async-start | bytes 393216 | tf_op jit(solution)/shard_map/all_to_all | solution.py:574
  11.2 0.2 collective-permute-start
  11.4 3.5 %collective-permute-start.1 = (f32[16,1024]{1,0:T(8,128)S(1)}, f32[16,1024]{1,0:T(8,128)S(1)}, u32[]{:S(2)}, u32[]{:S(2)}) collective-permute-start(f32[16,1024]{1,0:T(8,128)S(1)} %get-tuple-element.19), channel_id=1, source_target_pairs={{1,2},{3,4},{5,6},{7,8},{9,10},{11,12},{13,14},{2,1},{4,3},{6,5},{... | collective-permute-start | bytes 196616 | tf_op jit(solution)/shard_map/ppermute | solution.py:577
  14.9 0.0 collective-permute-done.halo_half
  14.9 3.5 %near_first.1 = (f32[16,2048]{1,0:T(8,128)S(1)}, bf16[2,16,32,128]{3,2,1,0:T(8,128)(2,1)S(1)}, s32[4,16]{1,0:T(4,128)S(1)}, f32[6,9,64,64]{3,2,1,0:T(8,128)S(1)}) custom-call(f32[16,1024]{1,0:T(8,128)S(1)} %collective-permute-done.halo_half, f32[16,2048]{1,0:T(8,128)} %vec_far.5, s32[9,32]{1,0:T(8,128)} %bitcast.14, s32[1,32]{1,0:T(1,128)} %bitcast.18, ...), custom_call_target="tpu_custom_call" | custom-call | flops 268435456 | bytes 16777216 | tf_op jit(solution)/shard_map/near_first/pallas_call | solution.py:597
  18.4 0.0 collective-permute-done.1.halo_half
  18.4 2.7 %near_second.1.near = f32[16,2048]{1,0:T(8,128)S(1)} custom-call(f32[16,1024]{1,0:T(8,128)S(1)} %collective-permute-done.1.halo_half, f32[16,2048]{1,0:T(8,128)} %vec_far.5, s32[9,32]{1,0:T(8,128)} %bitcast.15, s32[1,32]{1,0:T(1,128)} %bitcast.19, f32[32,9,64,64]{3,2,1,0:T(8,128)} %near_mat_far.3, ...), custom_call_target="tpu_custom_call", output_to_operand_aliasing={{}: (5, {})} | custom-call | flops 268435456 | bytes 8388608 | tf_op jit(solution)/shard_map/near_second/pallas_call | solution.py:622
  21.2 0.0 all-to-all-done.incoming
  21.2 2.5 %down.1 = f32[16,2048]{1,0:T(8,128)} custom-call(f32[16,24,128]{2,1,0:T(8,128)S(1)} %all-to-all-done.incoming, bf16[2,16,32,128]{3,2,1,0:T(8,128)(2,1)S(1)} %get-tuple-element.16.coup, bf16[2,4,32,128]{3,2,1,0:T(8,128)(2,1)S(1)} %get-tuple-element.17.upper, bf16[4,8,128,128]{3,2,1,0:T(8,128)(2,1)S(1)} %get-tuple-element.18.weights, ...), custom_call_target="tpu_custom_call" | custom-call | tf_op jit(solution)/shard_map/down/pallas_call | solution.py:634
Async XLA Ops:
  3.9 17.3 %all-to-all-start = ((f32[16,24,128]{2,1,0:T(8,128)}), f32[16,24,128]{2,1,0:T(8,128)S(1)}, u32[]{:S(2)}, u32[]{:S(2)}) async-start(f32[16,24,128]{2,1,0:T(8,128)} %get-tuple-element.14), calls=%async_computation | async-start | bytes 393216 | tf_op jit(solution)/shard_map/all_to_all | solution.py:574
  11.2 3.7 %collective-permute-start = (f32[16,1024]{1,0:T(8,128)S(1)}, f32[16,1024]{1,0:T(8,128)S(1)}, u32[]{:S(2)}, u32[]{:S(2)}) collective-permute-start(f32[16,1024]{1,0:T(8,128)S(1)} %get-tuple-element.15), channel_id=1, source_target_pairs={{0,1},{1,0},{2,3},{3,2},{4,5},{5,4},{6,7},{7,6},{8,9},{9,8},{10,11... | collective-permute-start | bytes 196616 | tf_op jit(solution)/shard_map/ppermute | solution.py:575
  11.4 7.1 %collective-permute-start.1 = (f32[16,1024]{1,0:T(8,128)S(1)}, f32[16,1024]{1,0:T(8,128)S(1)}, u32[]{:S(2)}, u32[]{:S(2)}) collective-permute-start(f32[16,1024]{1,0:T(8,128)S(1)} %get-tuple-element.19), channel_id=1, source_target_pairs={{1,2},{3,4},{5,6},{7,8},{9,10},{11,12},{13,14},{2,1},{4,3},{6,5},{... | collective-permute-start | bytes 196616 | tf_op jit(solution)/shard_map/ppermute | solution.py:577

commit v6 on v5

--- a/solution.py
+++ b/solution.py
@@ -303,8 +303,6 @@
         ahead_copy = pltpu.make_async_copy(others, ahead, semaphores.at[len(arriving)])
         ahead_copy.start()
     before()
-    for copy in arriving:
-        copy.wait()
     left = lane_part(vecs, leaf_size) == 0
 
     def lay(base, block):
@@ -317,8 +315,10 @@
                 values[base + 2 * m + c, vecs:] = low
 
     lay(upper * (halo + leaf_dev), halo_half[...])
+    values[2 * leaf_dev] = jnp.zeros((2 * vecs, LANES), BF16)
+    for copy in arriving:
+        copy.wait()
     lay(halo, vec[...])
-    values[2 * leaf_dev] = jnp.zeros((2 * vecs, LANES), BF16)
     shift = halo - position * leaf_dev
     wide_left = lane_part(2 * vecs, leaf_size) == 0
 

time: 24 us -> 23.9 us (level)
  no operation moved by 1% of the time
where the time goes in v6:
time: 23.9 us; the launch traced here: 23.7 us
  Pallas kernels  12.6 us (53%)
  starting transfers between devices  11 us (46%)
    all_to_all x1, starting transfers between devices, body(): lax.all_to_all(outgoing, BRANCH, split_axis=0, concat_axis=0, tiled=True)  7.32 us
    pallas_call x1, Pallas kernels, body(): pl.pallas_call(functools.partial(up_kernel, members, slots), out_shape=[s...  3.88 us
    pallas_call x1, Pallas kernels, body(): pl.pallas_call(functools.partial(first_kernel, members, slots), out_shape...  3.52 us
    ppermute x1, starting transfers between devices, body(): lax.ppermute(cross_half, BRANCH, pairs + [(b, a) for a, b in pairs])  3.51 us
    pallas_call x1, Pallas kernels, body(): pl.pallas_call(second_kernel, out_shape=shape((vecs, points), F32), in_sp...  2.69 us
    pallas_call x1, Pallas kernels, body(): pl.pallas_call(functools.partial(down_kernel, members, slots), out_shape=...  2.53 us
  transfers between devices with their start and end apart: 3, of which 0 were waited for; matrix products, arithmetic and copies ran while one was open for 0% of the time, Pallas kernels for 26%

profile of v6, /device:TPU:1, one launch (start us, length us, event | category | flops | bytes accessed | tf_op | source)
XLA Modules:
  0.0 23.7 jit_solution(17078532604531137329)
XLA Ops:
  0.0 3.9 %up.1 = (f32[16,24,128]{2,1,0:T(8,128)}, f32[16,1024]{1,0:T(8,128)S(1)}, f32[16,1024]{1,0:T(8,128)S(1)}, bf16[4,8,128,128]{3,2,1,0:T(8,128)(2,1)S(1)}, bf16[2,4,32,128]{3,2,1,0:T(8,128)(2,1)S(1)}) custom-call(f32[16,2048]{1,0:T(8,128)} %vec_far.5, f32[32,32,64]{2,1,0:T(8,128)} %basis_far.1, f32[62,32,32]{2,1,0:T(8,128)} %bitcast.12, s32[4,16]{1,0:T(4,128)} %bitcast.16, ...), custom_call_target="tpu_custom_call" | custom-call | tf_op jit(solution)/shard_map/up/pallas_call | solution.py:540
  3.9 7.3 %all-to-all-start = ((f32[16,24,128]{2,1,0:T(8,128)}), f32[16,24,128]{2,1,0:T(8,128)S(1)}, u32[]{:S(2)}, u32[]{:S(2)}) async-start(f32[16,24,128]{2,1,0:T(8,128)} %get-tuple-element.14), calls=%async_computation | async-start | bytes 393216 | tf_op jit(solution)/shard_map/all_to_all | solution.py:574
  11.2 0.2 collective-permute-start
  11.4 3.5 %collective-permute-start.1 = (f32[16,1024]{1,0:T(8,128)S(1)}, f32[16,1024]{1,0:T(8,128)S(1)}, u32[]{:S(2)}, u32[]{:S(2)}) collective-permute-start(f32[16,1024]{1,0:T(8,128)S(1)} %get-tuple-element.19), channel_id=1, source_target_pairs={{1,2},{3,4},{5,6},{7,8},{9,10},{11,12},{13,14},{2,1},{4,3},{6,5},{... | collective-permute-start | bytes 196616 | tf_op jit(solution)/shard_map/ppermute | solution.py:577
  14.9 0.0 collective-permute-done.halo_half
  14.9 3.5 %near_first.1 = (f32[16,2048]{1,0:T(8,128)S(1)}, bf16[2,16,32,128]{3,2,1,0:T(8,128)(2,1)S(1)}, s32[4,16]{1,0:T(4,128)S(1)}, f32[6,9,64,64]{3,2,1,0:T(8,128)S(1)}) custom-call(f32[16,1024]{1,0:T(8,128)S(1)} %collective-permute-done.halo_half, f32[16,2048]{1,0:T(8,128)} %vec_far.5, s32[9,32]{1,0:T(8,128)} %bitcast.14, s32[1,32]{1,0:T(1,128)} %bitcast.18, ...), custom_call_target="tpu_custom_call" | custom-call | flops 268435456 | bytes 16777216 | tf_op jit(solution)/shard_map/near_first/pallas_call | solution.py:597
  18.4 0.0 collective-permute-done.1.halo_half
  18.4 2.7 %near_second.1.near = f32[16,2048]{1,0:T(8,128)S(1)} custom-call(f32[16,1024]{1,0:T(8,128)S(1)} %collective-permute-done.1.halo_half, f32[16,2048]{1,0:T(8,128)} %vec_far.5, s32[9,32]{1,0:T(8,128)} %bitcast.15, s32[1,32]{1,0:T(1,128)} %bitcast.19, f32[32,9,64,64]{3,2,1,0:T(8,128)} %near_mat_far.3, ...), custom_call_target="tpu_custom_call", output_to_operand_aliasing={{}: (5, {})} | custom-call | flops 268435456 | bytes 8388608 | tf_op jit(solution)/shard_map/near_second/pallas_call | solution.py:622
  21.1 0.0 all-to-all-done.incoming
  21.2 2.5 %down.1 = f32[16,2048]{1,0:T(8,128)} custom-call(f32[16,24,128]{2,1,0:T(8,128)S(1)} %all-to-all-done.incoming, bf16[2,16,32,128]{3,2,1,0:T(8,128)(2,1)S(1)} %get-tuple-element.16.coup, bf16[2,4,32,128]{3,2,1,0:T(8,128)(2,1)S(1)} %get-tuple-element.17.upper, bf16[4,8,128,128]{3,2,1,0:T(8,128)(2,1)S(1)} %get-tuple-element.18.weights, ...), custom_call_target="tpu_custom_call" | custom-call | tf_op jit(solution)/shard_map/down/pallas_call | solution.py:634
Async XLA Ops:
  3.9 17.3 %all-to-all-start = ((f32[16,24,128]{2,1,0:T(8,128)}), f32[16,24,128]{2,1,0:T(8,128)S(1)}, u32[]{:S(2)}, u32[]{:S(2)}) async-start(f32[16,24,128]{2,1,0:T(8,128)} %get-tuple-element.14), calls=%async_computation | async-start | bytes 393216 | tf_op jit(solution)/shard_map/all_to_all | solution.py:574
  11.2 3.7 %collective-permute-start = (f32[16,1024]{1,0:T(8,128)S(1)}, f32[16,1024]{1,0:T(8,128)S(1)}, u32[]{:S(2)}, u32[]{:S(2)}) collective-permute-start(f32[16,1024]{1,0:T(8,128)S(1)} %get-tuple-element.15), channel_id=1, source_target_pairs={{0,1},{1,0},{2,3},{3,2},{4,5},{5,4},{6,7},{7,6},{8,9},{9,8},{10,11... | collective-permute-start | bytes 196616 | tf_op jit(solution)/shard_map/ppermute | solution.py:575
  11.4 7.1 %collective-permute-start.1 = (f32[16,1024]{1,0:T(8,128)S(1)}, f32[16,1024]{1,0:T(8,128)S(1)}, u32[]{:S(2)}, u32[]{:S(2)}) collective-permute-start(f32[16,1024]{1,0:T(8,128)S(1)} %get-tuple-element.19), channel_id=1, source_target_pairs={{1,2},{3,4},{5,6},{7,8},{9,10},{11,12},{13,14},{2,1},{4,3},{6,5},{... | collective-permute-start | bytes 196616 | tf_op jit(solution)/shard_map/ppermute | solution.py:577
